TPU v7x, 128 devices: a whole 4x4x4 slice. The times are simulated.
128 devices in a mesh: dp: 8 (over z, x_lo), ctx: 16 (over x_hi, y, core).
Axes of the slice: x: 4 (x_hi: 2, x_lo: 2; x = x_hi * 2 + x_lo), y: 4, z: 4, core: 2. Of those that a mesh axis runs over, the one named last changes fastest.
Arguments:
- queries: bfloat16 [8, 8192, 1536], P('dp', 'ctx'), may hold values from -6 to 6
- key_rows: bfloat16 [8, 8192, 1536], P('dp', 'ctx'), may hold values from -6 to 6
- values: bfloat16 [8, 8192, 1536], P('dp', 'ctx'), may hold values from -6 to 6
- saved_out: bfloat16 [8, 8192, 1536], P('dp', 'ctx'), may hold values from -6 to 6
- log_sum: float32 [8, 12, 8192], P('dp', None, 'ctx'), may hold values from 4 to 6
- out_grad: bfloat16 [8, 8192, 3072], P('dp', 'ctx'), may hold values from -6 to 6
- out_weight: bfloat16 [1536, 3072], P(('dp', 'ctx')), may hold values from -0.15625 to 0.15625
- tile_coords: int32 [64, 3], replicated, may hold values from 0 to 15, as said below
- extents: int32 [12, 3], replicated, may hold values from 0 to 1
Outputs:
- query_grad: bfloat16 [8, 8192, 1536], P('dp', 'ctx')
- key_grad: bfloat16 [8, 8192, 1536], P('dp', 'ctx')
- value_grad: bfloat16 [8, 8192, 1536], P('dp', 'ctx')
- weight_grad: float32 [1536, 3072], P(('dp', 'ctx'))
Inputs may be any that keep to these rules, and one draw needn't show every extreme that they name: `tile_coords`: row t belongs to tokens t * 128 to t * 128 + 127. Column 0 is the frame tile t // 4; columns 1 and 2 are a row below 2 and a column below 2; within each frame tile every pair of them appears once, in any order.
All inputs are finite; a program needn't handle non-finite values.
Results may differ from a plain program's by a relative error of at most 0.006.
Values may be sent and summed in bfloat16 or wider, within the bound.
A program may use at most 192 MiB of HBM per device.

v0:
```python
import math

import jax
import jax.numpy as jnp
from jax import lax
from jax.sharding import PartitionSpec as P

H = 12
HEAD = 128
TILE = 128


def padded_2(value, sides, width):
    for axis, dim in sides:
        size, length = (lax.axis_size(axis), value.shape[dim])
        up = [(i, (i + 1) % size) for i in range(size - 1)]
        down = [(j, i) for i, j in up]
        last = lax.slice_in_dim(value, length - width, length, axis=dim)
        initial = lax.slice_in_dim(value, 0, width, axis=dim)
        before = lax.ppermute(last, axis, up)
        after = lax.ppermute(initial, axis, down)
        value = jnp.concatenate([before, value, after], axis=dim)
    return value


def shifted(value, axis, steps):
    count = lax.axis_size(axis)
    initial, last = (max(0, -steps), min(count, count - steps))
    return lax.ppermute(value, axis, [(source, source + steps) for source in range(initial, last)])


def reach(row_coords, col_coords, spans):
    gap = jnp.abs(row_coords[:, None, :] - col_coords[None, :, :])
    return jnp.all(gap <= spans, axis=-1)


def softmax_grads(q_rows, a_rows, lse_rows, delta_rows, k_cols, v_cols, allowed, score_scale):
    scores = (
        jnp.einsum("bid,bjd->bij", q_rows, k_cols, preferred_element_type=jnp.float32) * score_scale
    )
    probs = jnp.where(allowed, jnp.exp(scores - lse_rows[:, :, None]), 0.0)
    d_probs = jnp.einsum("bid,bjd->bij", a_rows, v_cols, preferred_element_type=jnp.float32)
    d_scores = (probs * (d_probs - delta_rows[:, :, None])).astype(jnp.bfloat16)
    return (probs.astype(jnp.bfloat16), d_scores)


def head_slice(array, head):
    return lax.dynamic_slice_in_dim(array, head * HEAD, HEAD, array.ndim - 1)


def heads_last(stacked):
    count, clips_dev, rows_dev, width = stacked.shape
    return jnp.moveaxis(stacked, 0, 2).reshape(clips_dev, rows_dev, count * width)


def shards(
    queries, key_rows, values, saved_out, log_sum, out_grad, out_weight, tile_coords, extents
):
    clips_dev, tok_dev, features = queries.shape
    score_scale = HEAD ** (-0.5)
    position = lax.axis_index("ctx")
    tiles_dev = tok_dev // TILE
    d_attn = jnp.einsum(
        "btd,rd->btr",
        out_grad,
        lax.all_gather(out_weight, ("dp", "ctx"), axis=0, tiled=True),
        preferred_element_type=jnp.float32,
    ).astype(jnp.bfloat16)
    attn_wide = lax.optimization_barrier(d_attn).astype(jnp.float32)
    delta = jnp.sum(
        (attn_wide * saved_out.astype(jnp.float32)).reshape(clips_dev, tok_dev, H, HEAD), axis=-1
    )
    delta = delta.transpose(0, 2, 1)
    far = jnp.full((tiles_dev, 3), 1 << 20, jnp.int32)
    padded = jnp.concatenate([far, tile_coords, far], axis=0)
    own_coords = jnp.repeat(
        lax.dynamic_slice_in_dim(padded, (position + 1) * tiles_dev, tiles_dev, 0), TILE, axis=0
    )
    near_coords = jnp.repeat(
        lax.dynamic_slice_in_dim(padded, position * tiles_dev, 3 * tiles_dev, 0), TILE, axis=0
    )
    head_ids = jnp.arange(H, dtype=jnp.int32)
    paired = jnp.stack([key_rows, values])
    widened = padded_2(paired, (("ctx", 2),), tok_dev)

    def per_head(head):
        spans = lax.dynamic_index_in_dim(extents, head, 0, keepdims=False)
        q_head = head_slice(queries, head)
        a_head = head_slice(d_attn, head)
        k_near = head_slice(widened[0], head)
        v_near = head_slice(widened[1], head)
        lse_head = lax.dynamic_index_in_dim(log_sum, head, 1, keepdims=False)
        delta_head = lax.dynamic_index_in_dim(delta, head, 1, keepdims=False)
        allowed = reach(own_coords, near_coords, spans)
        probs, d_scores = softmax_grads(
            q_head, a_head, lse_head, delta_head, k_near, v_near, allowed, score_scale
        )
        query_part = (
            score_scale
            * jnp.einsum("bij,bjd->bid", d_scores, k_near, preferred_element_type=jnp.float32)
        ).astype(jnp.bfloat16)
        key_terms = score_scale * jnp.einsum(
            "bij,bid->bjd", d_scores, q_head, preferred_element_type=jnp.float32
        )
        value_terms = jnp.einsum("bij,bid->bjd", probs, a_head, preferred_element_type=jnp.float32)
        return (query_part, key_terms, value_terms)

    query_parts, key_terms, value_terms = lax.map(per_head, head_ids)
    query_grad = heads_last(query_parts)
    key_terms = heads_last(key_terms)
    value_terms = heads_last(value_terms)
    backward = jnp.stack([key_terms[:, :tok_dev], value_terms[:, :tok_dev]]).astype(jnp.bfloat16)
    onward = jnp.stack([key_terms[:, 2 * tok_dev :], value_terms[:, 2 * tok_dev :]]).astype(
        jnp.bfloat16
    )
    from_next = shifted(backward, "ctx", -1)
    from_prev = shifted(onward, "ctx", 1)
    key_grad = (
        key_terms[:, tok_dev : 2 * tok_dev]
        + from_next[0].astype(jnp.float32)
        + from_prev[0].astype(jnp.float32)
    ).astype(jnp.bfloat16)
    value_grad = (
        value_terms[:, tok_dev : 2 * tok_dev]
        + from_next[1].astype(jnp.float32)
        + from_prev[1].astype(jnp.float32)
    ).astype(jnp.bfloat16)
    norm = 1.0 / math.sqrt(clips_dev * lax.axis_size("dp") * tok_dev * lax.axis_size("ctx"))
    weight_grad = lax.psum_scatter(
        jnp.einsum("btr,btd->rd", saved_out, out_grad, preferred_element_type=jnp.float32) * norm,
        ("dp", "ctx"),
        scatter_dimension=0,
        tiled=True,
    )
    return (query_grad, key_grad, value_grad, weight_grad)


def solution(mesh):
    return jax.shard_map(
        shards,
        mesh=mesh,
        in_specs=(
            P("dp", "ctx", None),
            P("dp", "ctx", None),
            P("dp", "ctx", None),
            P("dp", "ctx", None),
            P("dp", None, "ctx"),
            P("dp", "ctx", None),
            P(("dp", "ctx"), None),
            P(),
            P(),
        ),
        out_specs=(
            P("dp", "ctx", None),
            P("dp", "ctx", None),
            P("dp", "ctx", None),
            P(("dp", "ctx"), None),
        ),
        check_vma=False,
    )
```

profile of v0, /device:TPU:4, one launch (start us, length us, event | category | flops | bytes accessed | tf_op | source)
XLA Modules:
  0.0 1281.9 jit_solution(12712622366600273414)
XLA Ops:
  18.5 10.7 convolution_multiply_fusion.3
  29.3 38.0 %collective-permute-done.1 = bf16[2,1,512,1536]{3,2,1,0:T(8,128)(2,1)} collective-permute-done((bf16[2,1,512,1536]{3,2,1,0:T(8,128)(2,1)}, bf16[2,1,512,1536]{3,2,1,0:T(8,128)(2,1)}, u32[]{:S(2)}, u32[]{:S(2)}) %collective-permute-start.1) | collective-permute-done | bytes 3145760 | tf_op jit(solution)/shard_map/ppermute | solution.py:21
  67.3 9.6 collective-permute-done
  76.9 7.0 pad_maximum_fusion
  83.9 138.8 %all-gather.3.cloned.1.call-done = bf16[128,12,3072]{2,1,0:T(8,128)(2,1)} async-done(((bf16[1,12,3072]{2,1,0:T(8,128)(2,1)}), bf16[128,12,3072]{2,1,0:T(8,128)(2,1)}) %all-gather.3.cloned.1.call-update) | async-done | bytes 9437200 | tf_op jit(solution)/shard_map/all_gather | solution.py:66
  222.8 13.7 %reshape.230 = bf16[1536,3072]{1,0:T(8,128)(2,1)} reshape(bf16[128,12,3072]{2,1,0:T(8,128)(2,1)} %all-gather.3.cloned.1.call-done) | data formatting | bytes 18874368
  236.5 7.9 fusion.46
  250.5 374.9 %while.15 = (s32[]{:T(128)}, bf16[12,1,512,128]{2,3,0,1:T(8,128)(2,1)}, f32[12,1,1536,128]{2,3,0,1:T(8,128)}, f32[12,1,1536,128]{2,3,0,1:T(8,128)}, s32[12]{0:T(...) while((s32[]{:T(128)}, ...), condition=%wide.region_3.4_spmd.clone, body=%wide.region_1.3_spmd.clone.sunk | while | flops 1021116416 | bytes 66959944 | solution.py:108
  256.4 8.0 fusion.84
  287.7 8.0 fusion.84
  318.9 8.0 fusion.84
  350.1 8.0 fusion.84
  381.3 8.0 fusion.84
  412.5 8.0 fusion.84
  443.7 8.0 fusion.84
  474.9 8.0 fusion.84
  506.1 8.0 fusion.84
  537.4 8.0 fusion.84
  568.6 8.0 fusion.84
  599.9 8.0 fusion.84
  625.3 7.1 bitcast_convert_fusion
  638.7 7.2 collective-permute-start.2
  645.9 352.9 %fusion.4 = f32[16,3072]{1,0:T(8,128)S(1)} fusion(f32[1536,3072]{1,0:T(8,128)} %convolution_multiply_fusion.3), kind=kCustom, calls=%all-reduce-scatter | all-reduce-scatter fusion | flops 6291457 | bytes 19070976
  1006.6 16.0 %collective-permute-start.32 = (f32[16,3072]{1,0:T(8,128)S(1)}, f32[16,3072]{1,0:T(8,128)S(1)}, u32[]{:S(2)}, u32[]{:S(2)}) collective-permute-start(f32[16,3072]{1,0:T(8,128)S(1)} %fusion.4), channel_id=1, source_target_pairs={{0,29},{1,30},{2,31},{3,32},{4,33},{5,34},{6,35},{7,36},{8,37},{9,... | collective-permute-start | bytes 589832
  1022.6 16.9 %collective-permute-start.31 = (f32[16,3072]{1,0:T(8,128)S(1)}, f32[16,3072]{1,0:T(8,128)S(1)}, u32[]{:S(2)}, u32[]{:S(2)}) collective-permute-start(f32[16,3072]{1,0:T(8,128)S(1)} %fusion.4), channel_id=1, source_target_pairs={{0,28},{1,29},{2,30},{3,31},{4,32},{5,33},{6,34},{7,35},{8,36},{9,... | collective-permute-start | bytes 589832
  1102.0 6.6 collective-permute-start.16
  1113.3 5.4 collective-permute-start.14
  1118.7 7.4 collective-permute-start.13
  1131.4 7.5 collective-permute-start.10
  1147.5 5.8 collective-permute-start.7
  1174.0 86.0 %concatenate.26 = f32[524,3072]{1,0:T(8,128)} concatenate(f32[12,3072]{1,0:T(8,128)} %copy-done.8, f32[16,3072]{1,0:T(8,128)S(1)} %collective-permute-done.34, f32[16,3072]{1,0:T(8,128)} %copy-done.9, f32[16,3072]{1,0:T(8,128)} %copy-done.10, f32[16,3072]{1,0:T(8,128)} %copy-done.11, f32[16,3072]{1,0:T(8,128)} %copy-done.12, f32[16,3072]{1,0:T(8,128)} %copy-done.13, ...), dimensions={0} | concatenate | bytes 12877824
  1264.2 5.6 fusion.37
  (422 shorter events, 388.7 us)
Async XLA Ops:
  7.2 215.6 %all-gather.3.cloned.1.call-start = ((), (), s32[]{:S(2)}) async-start(), calls=%async_computation | async-start | bytes 12681216 | tf_op jit(solution)/shard_map/all_gather | solution.py:66
  11.9 55.4 %collective-permute-start.1 = (bf16[2,1,512,1536]{3,2,1,0:T(8,128)(2,1)}, bf16[2,1,512,1536]{3,2,1,0:T(8,128)(2,1)}, u32[]{:S(2)}, u32[]{:S(2)}) collective-permute-start(bf16[2,1,512,1536]{3,2,1,0:T(8,128)(2,1)} %pad_maximum_fusion.1), channel_id=1, source_target_pairs={{1,0},{2,1},{3,2},{4,3},{5,4},{6,5},{7,6},{8,7},{9,8},{10,9},{11,1... | collective-permute-start | bytes 9437192 | tf_op jit(solution)/shard_map/ppermute | solution.py:21
  16.2 60.7 %collective-permute-start = (bf16[2,1,512,1536]{3,2,1,0:T(8,128)(2,1)}, bf16[2,1,512,1536]{3,2,1,0:T(8,128)(2,1)}, u32[]{:S(2)}, u32[]{:S(2)}) collective-permute-start(bf16[2,1,512,1536]{3,2,1,0:T(8,128)(2,1)} %pad_maximum_fusion.1), channel_id=1, source_target_pairs={{0,1},{1,2},{2,3},{3,4},{4,5},{5,6},{6,7},{7,8},{8,9},{9,10},{10,1... | collective-permute-start | bytes 9437192 | tf_op jit(solution)/shard_map/ppermute | solution.py:20
  634.8 629.4 %collective-permute-start.3 = (bf16[2,1,512,1536]{2,3,1,0:T(8,128)(2,1)}, bf16[2,1,512,1536]{2,3,1,0:T(8,128)(2,1)}, u32[]{:S(2)}, u32[]{:S(2)}) collective-permute-start(bf16[2,1,512,1536]{2,3,1,0:T(8,128)(2,1)} %pad_maximum_fusion.3), channel_id=1, source_target_pairs={{0,1},{1,2},{2,3},{3,4},{4,5},{5,6},{6,7},{7,8},{8,9},{9,10},{10,1... | collective-permute-start | bytes 9437192 | tf_op jit(solution)/shard_map/ppermute | solution.py:29
  638.7 625.5 %collective-permute-start.2 = (bf16[2,1,512,1536]{2,3,1,0:T(8,128)(2,1)}, bf16[2,1,512,1536]{2,3,1,0:T(8,128)(2,1)S(1)}, u32[]{:S(2)}, u32[]{:S(2)}) collective-permute-start(bf16[2,1,512,1536]{2,3,1,0:T(8,128)(2,1)} %pad_maximum_fusion.2), channel_id=1, source_target_pairs={{1,0},{2,1},{3,2},{4,3},{5,4},{6,5},{7,6},{8,7},{9,8},{10,9},{11,1... | collective-permute-start | bytes 9437192 | tf_op jit(solution)/shard_map/ppermute | solution.py:29
  998.8 23.7 %collective-permute-start.34 = (f32[16,3072]{1,0:T(8,128)S(1)}, f32[16,3072]{1,0:T(8,128)S(1)}, u32[]{:S(2)}, u32[]{:S(2)}) collective-permute-start(f32[16,3072]{1,0:T(8,128)S(1)} %fusion.4), channel_id=1, source_target_pairs={{0,31},{1,32},{2,33},{3,34},{4,35},{5,36},{6,37},{7,38},{8,39},{9,... | collective-permute-start | bytes 589832
  1001.5 38.0 %collective-permute-start.33 = (f32[16,3072]{1,0:T(8,128)S(1)}, f32[16,3072]{1,0:T(8,128)S(1)}, u32[]{:S(2)}, u32[]{:S(2)}) collective-permute-start(f32[16,3072]{1,0:T(8,128)S(1)} %fusion.4), channel_id=1, source_target_pairs={{0,30},{1,31},{2,32},{3,33},{4,34},{5,35},{6,36},{7,37},{8,38},{9,... | collective-permute-start | bytes 589832
  1006.6 35.5 %collective-permute-start.32 = (f32[16,3072]{1,0:T(8,128)S(1)}, f32[16,3072]{1,0:T(8,128)S(1)}, u32[]{:S(2)}, u32[]{:S(2)}) collective-permute-start(f32[16,3072]{1,0:T(8,128)S(1)} %fusion.4), channel_id=1, source_target_pairs={{0,29},{1,30},{2,31},{3,32},{4,33},{5,34},{6,35},{7,36},{8,37},{9,... | collective-permute-start | bytes 589832
  1022.6 22.6 %collective-permute-start.31 = (f32[16,3072]{1,0:T(8,128)S(1)}, f32[16,3072]{1,0:T(8,128)S(1)}, u32[]{:S(2)}, u32[]{:S(2)}) collective-permute-start(f32[16,3072]{1,0:T(8,128)S(1)} %fusion.4), channel_id=1, source_target_pairs={{0,28},{1,29},{2,30},{3,31},{4,32},{5,33},{6,34},{7,35},{8,36},{9,... | collective-permute-start | bytes 589832
  1042.1 13.4 %collective-permute-start.29 = (f32[16,3072]{1,0:T(8,128)S(1)}, f32[16,3072]{1,0:T(8,128)S(1)}, u32[]{:S(2)}, u32[]{:S(2)}) collective-permute-start(f32[16,3072]{1,0:T(8,128)S(1)} %fusion.4), channel_id=1, source_target_pairs={{0,26},{1,27},{2,28},{3,29},{4,30},{5,31},{6,32},{7,33},{8,34},{9,... | collective-permute-start | bytes 589832
  1045.1 15.1 %collective-permute-start.28 = (f32[16,3072]{1,0:T(8,128)S(1)}, f32[16,3072]{1,0:T(8,128)S(1)}, u32[]{:S(2)}, u32[]{:S(2)}) collective-permute-start(f32[16,3072]{1,0:T(8,128)S(1)} %fusion.4), channel_id=1, source_target_pairs={{0,25},{1,26},{2,27},{3,28},{4,29},{5,30},{6,31},{7,32},{8,33},{9,... | collective-permute-start | bytes 589832
  1050.7 14.4 %collective-permute-start.27 = (f32[16,3072]{1,0:T(8,128)S(1)}, f32[16,3072]{1,0:T(8,128)S(1)}, u32[]{:S(2)}, u32[]{:S(2)}) collective-permute-start(f32[16,3072]{1,0:T(8,128)S(1)} %fusion.4), channel_id=1, source_target_pairs={{0,24},{1,25},{2,26},{3,27},{4,28},{5,29},{6,30},{7,31},{8,32},{9,... | collective-permute-start | bytes 589832
  1055.5 13.8 %collective-permute-start.26 = (f32[16,3072]{1,0:T(8,128)S(1)}, f32[16,3072]{1,0:T(8,128)S(1)}, u32[]{:S(2)}, u32[]{:S(2)}) collective-permute-start(f32[16,3072]{1,0:T(8,128)S(1)} %fusion.4), channel_id=1, source_target_pairs={{0,23},{1,24},{2,25},{3,26},{4,27},{5,28},{6,29},{7,30},{8,31},{9,... | collective-permute-start | bytes 589832
  1060.3 14.6 %collective-permute-start.25 = (f32[16,3072]{1,0:T(8,128)S(1)}, f32[16,3072]{1,0:T(8,128)S(1)}, u32[]{:S(2)}, u32[]{:S(2)}) collective-permute-start(f32[16,3072]{1,0:T(8,128)S(1)} %fusion.4), channel_id=1, source_target_pairs={{0,22},{1,23},{2,24},{3,25},{4,26},{5,27},{6,28},{7,29},{8,30},{9,... | collective-permute-start | bytes 589832
  1065.1 15.1 %collective-permute-start.24 = (f32[16,3072]{1,0:T(8,128)S(1)}, f32[16,3072]{1,0:T(8,128)S(1)}, u32[]{:S(2)}, u32[]{:S(2)}) collective-permute-start(f32[16,3072]{1,0:T(8,128)S(1)} %fusion.4), channel_id=1, source_target_pairs={{0,21},{1,22},{2,23},{3,24},{4,25},{5,26},{6,27},{7,28},{8,29},{9,... | collective-permute-start | bytes 589832
  1069.4 14.9 %collective-permute-start.23 = (f32[16,3072]{1,0:T(8,128)S(1)}, f32[16,3072]{1,0:T(8,128)S(1)}, u32[]{:S(2)}, u32[]{:S(2)}) collective-permute-start(f32[16,3072]{1,0:T(8,128)S(1)} %fusion.4), channel_id=1, source_target_pairs={{0,20},{1,21},{2,22},{3,23},{4,24},{5,25},{6,26},{7,27},{8,28},{9,... | collective-permute-start | bytes 589832
  1074.9 14.4 %collective-permute-start.22 = (f32[16,3072]{1,0:T(8,128)S(1)}, f32[16,3072]{1,0:T(8,128)S(1)}, u32[]{:S(2)}, u32[]{:S(2)}) collective-permute-start(f32[16,3072]{1,0:T(8,128)S(1)} %fusion.4), channel_id=1, source_target_pairs={{0,19},{1,20},{2,21},{3,22},{4,23},{5,24},{6,25},{7,26},{8,27},{9,... | collective-permute-start | bytes 589832
  1080.3 13.3 %collective-permute-start.21 = (f32[16,3072]{1,0:T(8,128)S(1)}, f32[16,3072]{1,0:T(8,128)S(1)}, u32[]{:S(2)}, u32[]{:S(2)}) collective-permute-start(f32[16,3072]{1,0:T(8,128)S(1)} %fusion.4), channel_id=1, source_target_pairs={{0,18},{1,19},{2,20},{3,21},{4,22},{5,23},{6,24},{7,25},{8,26},{9,... | collective-permute-start | bytes 589832
  1084.3 13.5 %collective-permute-start.20 = (f32[16,3072]{1,0:T(8,128)S(1)}, f32[16,3072]{1,0:T(8,128)S(1)}, u32[]{:S(2)}, u32[]{:S(2)}) collective-permute-start(f32[16,3072]{1,0:T(8,128)S(1)} %fusion.4), channel_id=1, source_target_pairs={{0,17},{1,18},{2,19},{3,20},{4,21},{5,22},{6,23},{7,24},{8,25},{9,... | collective-permute-start | bytes 589832
  1093.6 15.1 %collective-permute-start.18 = (f32[16,3072]{1,0:T(8,128)S(1)}, f32[16,3072]{1,0:T(8,128)S(1)}, u32[]{:S(2)}, u32[]{:S(2)}) collective-permute-start(f32[16,3072]{1,0:T(8,128)S(1)} %fusion.4), channel_id=1, source_target_pairs={{0,15},{1,16},{2,17},{3,18},{4,19},{5,20},{6,21},{7,22},{8,23},{9,... | collective-permute-start | bytes 589832
  1097.8 15.5 %collective-permute-start.17 = (f32[16,3072]{1,0:T(8,128)S(1)}, f32[16,3072]{1,0:T(8,128)S(1)}, u32[]{:S(2)}, u32[]{:S(2)}) collective-permute-start(f32[16,3072]{1,0:T(8,128)S(1)} %fusion.4), channel_id=1, source_target_pairs={{0,14},{1,15},{2,16},{3,17},{4,18},{5,19},{6,20},{7,21},{8,22},{9,... | collective-permute-start | bytes 589832
  1102.0 16.7 %collective-permute-start.16 = (f32[16,3072]{1,0:T(8,128)S(1)}, f32[16,3072]{1,0:T(8,128)S(1)}, u32[]{:S(2)}, u32[]{:S(2)}) collective-permute-start(f32[16,3072]{1,0:T(8,128)S(1)} %fusion.4), channel_id=1, source_target_pairs={{0,13},{1,14},{2,15},{3,16},{4,17},{5,18},{6,19},{7,20},{8,21},{9,... | collective-permute-start | bytes 589832
  1108.6 17.6 %collective-permute-start.15 = (f32[16,3072]{1,0:T(8,128)S(1)}, f32[16,3072]{1,0:T(8,128)S(1)}, u32[]{:S(2)}, u32[]{:S(2)}) collective-permute-start(f32[16,3072]{1,0:T(8,128)S(1)} %fusion.4), channel_id=1, source_target_pairs={{0,12},{1,13},{2,14},{3,15},{4,16},{5,17},{6,18},{7,19},{8,20},{9,... | collective-permute-start | bytes 589832
  1113.3 14.2 %collective-permute-start.14 = (f32[16,3072]{1,0:T(8,128)S(1)}, f32[16,3072]{1,0:T(8,128)S(1)}, u32[]{:S(2)}, u32[]{:S(2)}) collective-permute-start(f32[16,3072]{1,0:T(8,128)S(1)} %fusion.4), channel_id=1, source_target_pairs={{0,11},{1,12},{2,13},{3,14},{4,15},{5,16},{6,17},{7,18},{8,19},{9,... | collective-permute-start | bytes 589832
  1118.7 12.7 collective-permute-start.13
  1126.2 12.7 collective-permute-start.12
  1127.5 16.1 %collective-permute-start.11 = (f32[16,3072]{1,0:T(8,128)S(1)}, f32[16,3072]{1,0:T(8,128)S(1)}, u32[]{:S(2)}, u32[]{:S(2)}) collective-permute-start(f32[16,3072]{1,0:T(8,128)S(1)} %fusion.4), channel_id=1, source_target_pairs={{0,8},{1,9},{2,10},{3,11},{4,12},{5,13},{6,14},{7,15},{8,16},{9,17... | collective-permute-start | bytes 589832
  1131.4 16.1 %collective-permute-start.10 = (f32[16,3072]{1,0:T(8,128)S(1)}, f32[16,3072]{1,0:T(8,128)S(1)}, u32[]{:S(2)}, u32[]{:S(2)}) collective-permute-start(f32[16,3072]{1,0:T(8,128)S(1)} %fusion.4), channel_id=1, source_target_pairs={{0,7},{1,8},{2,9},{3,10},{4,11},{5,12},{6,13},{7,14},{8,15},{9,16}... | collective-permute-start | bytes 589832
  1138.9 14.5 %collective-permute-start.9 = (f32[16,3072]{1,0:T(8,128)S(1)}, f32[16,3072]{1,0:T(8,128)S(1)}, u32[]{:S(2)}, u32[]{:S(2)}) collective-permute-start(f32[16,3072]{1,0:T(8,128)S(1)} %fusion.4), channel_id=1, source_target_pairs={{0,6},{1,7},{2,8},{3,9},{4,10},{5,11},{6,12},{7,13},{8,14},{9,15},... | collective-permute-start | bytes 589832
  1147.5 14.8 %collective-permute-start.7 = (f32[16,3072]{1,0:T(8,128)S(1)}, f32[16,3072]{1,0:T(8,128)S(1)}, u32[]{:S(2)}, u32[]{:S(2)}) collective-permute-start(f32[16,3072]{1,0:T(8,128)S(1)} %fusion.4), channel_id=1, source_target_pairs={{0,4},{1,5},{2,6},{3,7},{4,8},{5,9},{6,10},{7,11},{8,12},{9,13},{1... | collective-permute-start | bytes 589832
  1153.4 12.7 collective-permute-start.6
  1155.3 15.1 %collective-permute-start.5 = (f32[16,3072]{1,0:T(8,128)S(1)}, f32[16,3072]{1,0:T(8,128)}, u32[]{:S(2)}, u32[]{:S(2)}) collective-permute-start(f32[16,3072]{1,0:T(8,128)S(1)} %fusion.4), channel_id=1, source_target_pairs={{0,2},{1,3},{2,4},{3,5},{4,6},{5,7},{6,8},{7,9},{8,10},{9,11},{10,... | collective-permute-start | bytes 589832
  (65 other events, 2209.5 us)
Sparse Core Ops, SparseCore 0:
  9.7 212.9 all-gather.2
where the time goes:
time: 1290 us; the launch traced here: 1280 us
  blocking collectives  353 us (27%)
  local copies, waits for them, and re-layouts  310 us (24%)
  waiting for transfers between devices  229 us (18%)
  starting transfers between devices  148 us (11%)
  matrix products  137 us (11%)
  other arithmetic  58.6 us (5%)
  loops' own time  32.3 us (3%)
  between operations  15 us (1%)
    unnamed x1, blocking collectives  353 us
    all_gather x1, waiting for transfers between devices, shards(): lax.all_gather(out_weight, ('dp', 'ctx'), axis=0, tiled=True)  139 us
    unnamed x32, starting transfers between devices  133 us
    unnamed x80, local copies, waits for them, and re-layouts  111 us
    slice x12, local copies, waits for them, and re-layouts, per_head(): v_near = head_slice(widened[1], head)  95.7 us
    dynamic_update_slice x48, local copies, waits for them, and re-layouts, shards(): query_parts, key_terms, value_terms = lax.map(per_head, head_ids)  63.8 us
    unnamed x33, waiting for transfers between devices  42.3 us
    ppermute x1, waiting for transfers between devices, padded_2(): after = lax.ppermute(initial, axis, down)  38 us
  transfers between devices with their start and end apart: 37, of which 18 were waited for; matrix products, arithmetic and copies ran while one was open for 36% of the time, Pallas kernels for 0%

commit v1 on v0

v1 whole, which is shorter than its diff:
```python
import functools
import math

import jax
import jax.numpy as jnp
from jax import lax
from jax.experimental import pallas as pl
from jax.experimental.pallas import tpu as pltpu
from jax.sharding import PartitionSpec as P

H = 12
HEAD = 128
TILE = 128
TOK = 512
HD = 1536
D = 3072
HALF = D // 2
ROWS = 12
PAD = 16
BLK = 8 * ROWS
CUT = 1024
PARTS = ((0, CUT), (CUT, HALF))
STEPS = (1, 3, 2)
MESH = pl.DeviceIdType.MESH
F32 = jnp.float32
BF16 = jnp.bfloat16
LOG2E = math.log2(math.e)
NT = (((1,), (1,)), ((), ()))
TN = (((0,), (0,)), ((), ()))


def place():
    dp, ctx = lax.axis_index("dp"), lax.axis_index("ctx")
    return dp // 2, (ctx // 8) * 2 + dp % 2, (ctx // 2) % 4, ctx % 2


def device(z, x, y, c):
    return (z * 2 + x % 2, (x // 2) * 8 + y * 2 + c)


def block_of(z, x):
    return z * 4 + (x % 2) * 2 + x // 2


def remote(src, dst, send, recv, target):
    return pltpu.make_async_remote_copy(
        src_ref=src, dst_ref=dst, send_sem=send, recv_sem=recv,
        device_id=target, device_id_type=MESH,
    )


def greet(z, x, y, c):
    ctx = lax.axis_index("ctx")
    dp = lax.axis_index("dp")
    barrier = pltpu.get_barrier_semaphore()

    def tell(target):
        pl.semaphore_signal(barrier, inc=1, device_id=target, device_id_type=MESH)

    for dy in range(4):
        for dc in range(2):
            if dy or dc:
                tell(device(z, x, (y + dy) % 4, (c + dc) % 2))
    for step in STEPS:
        tell(device(z, (x + step) % 4, y, c))
        tell(device((z + step) % 4, x, y, c))

    @pl.when(ctx == 7)
    def _():
        tell((dp, ctx + 1))

    @pl.when(ctx == 8)
    def _():
        tell((dp, ctx - 1))

    pl.semaphore_wait(barrier, 13 + jnp.where((ctx == 7) | (ctx == 8), 1, 0))


def halo_copies(pairs, send, recv):
    dp, ctx = lax.axis_index("dp"), lax.axis_index("ctx")
    up = jnp.minimum(ctx + 1, 15)
    down = jnp.maximum(ctx - 1, 0)
    half = len(pairs) // 2
    return [
        remote(src, dst, send.at[i], recv.at[i], (dp, up if i < half else down))
        for i, (src, dst) in enumerate(pairs)
    ]


def halo_start(copies):
    ctx = lax.axis_index("ctx")
    half = len(copies) // 2

    @pl.when(ctx < 15)
    def _():
        for copy in copies[:half]:
            copy.start()

    @pl.when(ctx > 0)
    def _():
        for copy in copies[half:]:
            copy.start()


def halo_wait(copies):
    ctx = lax.axis_index("ctx")
    half = len(copies) // 2

    @pl.when(ctx < 15)
    def _():
        for copy in copies[:half]:
            copy.wait_send()
        for copy in copies[half:]:
            copy.wait_recv()

    @pl.when(ctx > 0)
    def _():
        for copy in copies[half:]:
            copy.wait_send()
        for copy in copies[:half]:
            copy.wait_recv()


def gather_kernel(
    strip, keys, vals, so, og,
    before, after, d_attn, wgrad,
    strips, full, so_sib, og_sib,
    strip_send, strip_recv, near_send, far_send, ag_recv, sib_send, sib_recv,
    ex_send, ex_recv, halo_send, halo_recv,
):
    z, x, y, c = place()
    sib = device(z, x, y, 1 - c)
    me = block_of(z, x)
    slot = y * 2 + c
    greet(z, x, y, c)

    pending = []
    number = 0
    for dy in range(4):
        for dc in range(2):
            if dy or dc:
                copy = remote(strip, strips.at[slot], strip_send.at[number], strip_recv.at[slot],
                              device(z, x, (y + dy) % 4, (c + dc) % 2))
                copy.start()
                pending.append(copy)
                number += 1
    other = pl.ds(pl.multiple_of((1 - c) * HALF, HALF), HALF)
    exchange = [
        remote(so, so_sib, ex_send.at[0], ex_recv.at[0], sib),
        remote(og.at[:, other], og_sib, ex_send.at[1], ex_recv.at[1], sib),
    ]
    for copy in exchange:
        copy.start()
    halos = halo_copies(
        [(keys, before.at[0]), (vals, before.at[1]), (keys, after.at[0]), (vals, after.at[1])],
        halo_send, halo_recv)
    halo_start(halos)
    strips[slot] = strip[...]
    for dy in range(4):
        for dc in range(2):
            if dy or dc:
                src = ((y + dy) % 4) * 2 + (c + dc) % 2
                remote(strip, strips.at[src], strip_send.at[0], strip_recv.at[src], sib).wait_recv()
    row = lax.broadcasted_iota(jnp.int32, (BLK, 8 * PAD), 0)
    col = lax.broadcasted_iota(jnp.int32, (BLK, 8 * PAD), 1)
    pick = jnp.where(col == (row // ROWS) * PAD + row % ROWS, 1.0, 0.0).astype(BF16)
    for h in range(2):
        for o in range(0, HALF, 768):
            full[h, me, :, o:o + 768] = jnp.dot(
                pick, strips[:, :, h * HALF + o:h * HALF + o + 768].reshape(8 * PAD, 768),
                preferred_element_type=F32).astype(BF16)

    def piece(half, block, part):
        low, high = PARTS[part]
        return full.at[half, block, :, low:high]

    def along(part, first, step):
        over_x = (part == 0) == first
        return device(z, (x + step) % 4, y, c) if over_x else device((z + step) % 4, x, y, c)

    def block_at(part, first, step):
        if part == 0:
            return block_of(z, (x + step) % 4)
        return block_of((z + step) % 4, x)

    for part in range(2):
        for i, step in enumerate(STEPS):
            copy = remote(piece(c, me, part), piece(c, me, part), near_send.at[part, i],
                          ag_recv.at[part, me], along(part, True, step))
            copy.start()
            pending.append(copy)

    def onward(part, block, j):
        for i, step in enumerate(STEPS):
            copy = remote(piece(c, block, part), piece(c, block, part), far_send.at[part, j, i],
                          ag_recv.at[part, block], along(part, False, step))
            copy.start()
            pending.append(copy)

    def to_sibling(part, block):
        copy = remote(piece(c, block, part), piece(c, block, part), sib_send.at[part, block],
                      sib_recv.at[part, block], sib)
        copy.start()
        pending.append(copy)

    def arrived(part, block):
        remote(piece(c, block, part), piece(c, block, part), near_send.at[part, 0],
               ag_recv.at[part, block], sib).wait_recv()

    for part in range(2):
        onward(part, me, 0)

    for copy in exchange:
        copy.wait_recv()
    mine = pl.ds(pl.multiple_of(c * HALF, HALF), HALF)

    def wgrad_rows(i, carry):
        rows = pl.ds(pl.multiple_of(i * 256, 256), 256)
        total = lax.dot_general(so[:, rows], og[:, mine], TN, preferred_element_type=F32)
        total += lax.dot_general(so_sib[:, rows], og_sib[...], TN, preferred_element_type=F32)
        wgrad[rows, :] = total.astype(BF16)
        return carry

    for j, step in enumerate(STEPS):
        for part in range(2):
            block = block_at(part, True, step)
            arrived(part, block)
            onward(part, block, j + 1)
            to_sibling(part, block)
    lax.fori_loop(0, HD // 256, wgrad_rows, 0)

    for step in STEPS:
        for inner in (0,) + STEPS:
            block = block_of((z + step) % 4, (x + inner) % 4)
            arrived(0, block)
            to_sibling(0, block)
            block = block_of((z + inner) % 4, (x + step) % 4)
            arrived(1, block)
            to_sibling(1, block)

    for step in (0,) + STEPS:
        group = (z + step) % 4
        for inner in range(4):
            block = group * 4 + inner
            for part in range(2):
                @pl.when(block != me)
                def _():
                    remote(piece(1 - c, block, part), piece(1 - c, block, part),
                           sib_send.at[part, block], sib_recv.at[part, block], sib).wait_recv()
        feats = pl.ds(pl.multiple_of(group * 4 * BLK, 4 * BLK), 4 * BLK)

        def project(i, carry):
            rows = pl.ds(pl.multiple_of(i * 256, 256), 256)
            total = jnp.zeros((256, 4 * BLK), F32)
            for h in range(2):
                weight = full[h, pl.ds(group * 4, 4)].reshape(4 * BLK, HALF)
                total += lax.dot_general(og[rows, h * HALF:(h + 1) * HALF], weight, NT,
                                         preferred_element_type=F32)
            d_attn[rows, feats] = total.astype(BF16)
            return carry

        lax.fori_loop(0, TOK // 256, project, 0)
    halo_wait(halos)
    for copy in exchange:
        copy.wait_send()
    for copy in pending:
        copy.wait_send()


def scatter_kernel(
    wgrad, to_prev, to_next,
    out, from_next, from_prev,
    got_a, sum_a, got_b, sum_b, got_a2, got_b2, packed, last,
    first_send, first_recv, second_send, second_recv, last_send, last_recv, halo_send, halo_recv,
):
    z, x, y, c = place()
    slot = y * 2 + c
    greet(z, x, y, c)
    (a0, a1), (b0, b1) = PARTS
    pending = []
    for i, step in enumerate(STEPS):
        tz, tx = (z + step) % 4, (x + step) % 4
        for part, src, dst, target in (
            (0, wgrad.at[tz, :, :, a0:a1], got_a.at[i], device(tz, x, y, c)),
            (1, wgrad.at[:, (tx % 2) * 2 + tx // 2, :, b0:b1], got_b.at[i], device(z, tx, y, c)),
        ):
            copy = remote(src, dst, first_send.at[part, i], first_recv.at[part, i], target)
            copy.start()
            pending.append(copy)
    halos = halo_copies(
        [(to_next, from_prev), (to_prev, from_next)], halo_send, halo_recv)
    halo_start(halos)
    for i in range(3):
        pending[2 * i].wait_recv()
        pending[2 * i + 1].wait_recv()
    xs = (x % 2) * 2 + x // 2
    for j in range(4):
        total = wgrad[z, j, :, a0:a1].astype(F32)
        for i in range(3):
            total += got_a[i, j].astype(F32)
        sum_a[j] = total.astype(BF16)
        total = wgrad[j, xs, :, b0:b1].astype(F32)
        for i in range(3):
            total += got_b[i, j].astype(F32)
        sum_b[j] = total.astype(BF16)
    second = []
    for i, step in enumerate(STEPS):
        tz, tx = (z + step) % 4, (x + step) % 4
        for part, src, dst, target in (
            (0, sum_a.at[(tx % 2) * 2 + tx // 2], got_a2.at[i], device(z, tx, y, c)),
            (1, sum_b.at[tz], got_b2.at[i], device(tz, x, y, c)),
        ):
            copy = remote(src, dst, second_send.at[part, i], second_recv.at[part, i], target)
            copy.start()
            second.append(copy)
    for copy in second:
        copy.wait_recv()
    row = lax.broadcasted_iota(jnp.int32, (8 * PAD, BLK), 0)
    col = lax.broadcasted_iota(jnp.int32, (8 * PAD, BLK), 1)
    spread = jnp.where(
        (col == (row // PAD) * ROWS + row % PAD) & (row % PAD < ROWS), 1.0, 0.0).astype(BF16)
    total_a = sum_a[xs].astype(F32)
    total_b = sum_b[z].astype(F32)
    for i in range(3):
        total_a += got_a2[i].astype(F32)
        total_b += got_b2[i].astype(F32)
    packed[:, :, a0:a1] = jnp.dot(spread, total_a.astype(BF16), preferred_element_type=F32).astype(
        BF16).reshape(8, PAD, a1 - a0)
    packed[:, :, b0:b1] = jnp.dot(spread, total_b.astype(BF16), preferred_element_type=F32).astype(
        BF16).reshape(8, PAD, b1 - b0)
    number = 0
    third = []
    for dy in range(4):
        for dc in range(2):
            if dy or dc:
                ty, tc = (y + dy) % 4, (c + dc) % 2
                copy = remote(packed.at[ty * 2 + tc], last.at[slot], last_send.at[number],
                              last_recv.at[slot], device(z, x, ty, tc))
                copy.start()
                third.append(copy)
                number += 1
    last[slot] = packed[slot]
    for dy in range(4):
        for dc in range(2):
            if dy or dc:
                src = ((y + dy) % 4) * 2 + (c + dc) % 2
                remote(packed.at[src], last.at[src], last_send.at[0], last_recv.at[src],
                       device(z, x, y, 1 - c)).wait_recv()
    for h in range(2):
        total = last[h].astype(F32)
        for i in range(1, 4):
            total += last[2 * i + h].astype(F32)
        out[:, h * HALF:(h + 1) * HALF] = total * (1.0 / 256.0)
    halo_wait(halos)
    for copy in pending + second + third:
        copy.wait_send()


def attention_kernel(
    coords, extents,
    q_ref, k_ref, v_ref, kp_ref, vp_ref, kn_ref, vn_ref, a_ref, o_ref, lse_ref,
    dq_ref, dk_ref, dv_ref, prev_ref, next_ref,
    table, q_s, a_s, k_s, v_s, kt_s, row_s, dqt_s,
):
    head = pl.program_id(0)
    frame = lax.axis_index("ctx")
    scale = HEAD ** (-0.5)

    @pl.when(head == 0)
    def _():
        for k in range(3):
            base = jnp.clip(frame + k - 1, 0, 15) * 4
            for t in range(4):
                r, col = coords[base + t, 1], coords[base + t, 2]
                table[0, k, r * 2 + col] = t
                table[1, k, col * 2 + r] = t

    near_f, near_r, near_c = extents[head, 0], extents[head, 1], extents[head, 2]
    order = jnp.where(near_c == 0, 1, 0)

    def rows(k, s):
        return pl.ds(pl.multiple_of(table[order, k, s] * TILE, TILE), TILE)

    for s in range(4):
        own = rows(1, s)
        here = slice(s * TILE, (s + 1) * TILE)
        q_s[here, :] = q_ref[own, :]
        a_tile = a_ref[own, :]
        a_s[here, :] = a_tile
        prod = a_tile.astype(F32) * o_ref[own, :].astype(F32)
        row_s[0:1, here] = lse_ref[:, own] * LOG2E
        row_s[1:2, here] = jnp.sum(prod.T, axis=0, keepdims=True)
    sources = ((kp_ref, vp_ref), (k_ref, v_ref), (kn_ref, vn_ref))

    def load(k):
        for s in range(4):
            here = slice(s * TILE, (s + 1) * TILE)
            tile = sources[k][0][rows(k, s), :]
            k_s[k, here, :] = tile
            kt_s[k, :, here] = tile.T
            v_s[k, here, :] = sources[k][1][rows(k, s), :]

    def put(k, s, dk, dv):
        if k == 1:
            dk_ref[rows(k, s), :] = dk
            dv_ref[rows(k, s), :] = dv
        elif k == 0:
            prev_ref[0, rows(k, s), :] = dk.astype(BF16)
            prev_ref[1, rows(k, s), :] = dv.astype(BF16)
        else:
            next_ref[0, rows(k, s), :] = dk.astype(BF16)
            next_ref[1, rows(k, s), :] = dv.astype(BF16)

    def unit(k, begin, size):
        span = slice(begin, begin + size)
        q, a = q_s[span, :], a_s[span, :]
        lse, delta = row_s[0:1, span], row_s[1:2, span]
        step = min(size, 256)
        total = None
        for at in range(begin, begin + size, step):
            part = slice(at, at + step)
            scores = lax.dot_general(k_s[k, part, :], q, NT, preferred_element_type=F32)
            probs = jnp.exp2(scores * (scale * LOG2E) - lse)
            d_probs = lax.dot_general(v_s[k, part, :], a, NT, preferred_element_type=F32)
            d_scores = (probs * (d_probs - delta)).astype(BF16)
            dv = jnp.dot(probs.astype(BF16), a, preferred_element_type=F32)
            dk = jnp.dot(d_scores, q, preferred_element_type=F32) * scale
            dqt = jnp.dot(kt_s[k, :, part], d_scores, preferred_element_type=F32)
            total = dqt if total is None else total + dqt
            for i in range(step // TILE):
                cut = slice(i * TILE, (i + 1) * TILE)
                put(k, at // TILE + i, dk[cut], dv[cut])
        if k == 1:
            dqt_s[:, span] = total
        else:
            dqt_s[:, span] += total

    def frame_of(k):
        load(k)

        @pl.when(near_r * near_c == 1)
        def _():
            unit(k, 0, 512)

        @pl.when(near_r + near_c == 1)
        def _():
            for g in range(2):
                unit(k, g * 256, 256)

        @pl.when(near_r + near_c == 0)
        def _():
            for g in range(4):
                unit(k, g * 128, 128)

    frame_of(1)
    for k, there, ref in ((0, frame > 0, prev_ref), (2, frame < 15, next_ref)):
        use = (near_f == 1) & there

        @pl.when(use)
        def _():
            frame_of(k)

        @pl.when(jnp.logical_not(use))
        def _():
            ref[...] = jnp.zeros_like(ref)

    for s in range(4):
        dq_ref[rows(1, s), :] = (dqt_s[:, s * TILE:(s + 1) * TILE].T * scale).astype(BF16)


def any_spec():
    return pl.BlockSpec(memory_space=pl.ANY)


def vmem_spec():
    return pl.BlockSpec(memory_space=pltpu.VMEM)


def shards(
    queries, key_rows, values, saved_out, log_sum, out_grad, out_weight, tile_coords, extents
):
    q, k, v, so, og = (a[0] for a in (queries, key_rows, values, saved_out, out_grad))
    strip = jnp.pad(out_weight, ((0, PAD - ROWS), (0, 0)))
    dma = pltpu.SemaphoreType.DMA
    pair = jax.ShapeDtypeStruct((2, TOK, HD), BF16)
    before, after, d_attn, wgrad = pl.pallas_call(
        gather_kernel,
        out_shape=(pair, pair, jax.ShapeDtypeStruct((TOK, HD), BF16),
                   jax.ShapeDtypeStruct((HD, HALF), BF16)),
        in_specs=[vmem_spec(), any_spec(), any_spec(), vmem_spec(), vmem_spec()],
        out_specs=(any_spec(), any_spec(), vmem_spec(), vmem_spec()),
        scratch_shapes=[
            pltpu.VMEM((8, PAD, D), BF16),
            pltpu.VMEM((2, 16, BLK, HALF), BF16),
            pltpu.VMEM((TOK, HD), BF16),
            pltpu.VMEM((TOK, HALF), BF16),
            dma((7,)), dma((8,)), dma((2, 3)), dma((2, 4, 3)), dma((2, 16)), dma((2, 16)),
            dma((2, 16)), dma((2,)), dma((2,)), dma((4,)), dma((4,)),
        ],
        compiler_params=pltpu.CompilerParams(
            collective_id=0, has_side_effects=True, vmem_limit_bytes=48 * 2**20),
        name="gather",
    )(strip, k, v, so, og)

    def col():
        return pl.BlockSpec((TOK, HEAD), lambda h, *_: (0, h))

    def pair_col(i):
        return pl.BlockSpec((None, TOK, HEAD), lambda h, *_: (i, 0, h))

    both = pl.BlockSpec((2, TOK, HEAD), lambda h, *_: (0, 0, h))
    own32 = jax.ShapeDtypeStruct((TOK, HD), F32)
    own16 = jax.ShapeDtypeStruct((TOK, HD), BF16)
    dq, dk, dv, to_prev, to_next = pl.pallas_call(
        attention_kernel,
        out_shape=(own16, own32, own32, pair, pair),
        grid_spec=pltpu.PrefetchScalarGridSpec(
            num_scalar_prefetch=2,
            grid=(H,),
            in_specs=[col(), col(), col(), pair_col(0), pair_col(1), pair_col(0), pair_col(1),
                      col(), col(), pl.BlockSpec((None, 1, TOK), lambda h, *_: (h, 0, 0))],
            out_specs=(col(),) * 3 + (both,) * 2,
            scratch_shapes=[
                pltpu.SMEM((2, 3, 4), jnp.int32),
                pltpu.VMEM((TOK, HEAD), BF16),
                pltpu.VMEM((TOK, HEAD), BF16),
                pltpu.VMEM((3, TOK, HEAD), BF16),
                pltpu.VMEM((3, TOK, HEAD), BF16),
                pltpu.VMEM((3, HEAD, TOK), BF16),
                pltpu.VMEM((8, TOK), F32),
                pltpu.VMEM((HEAD, TOK), F32),
            ],
        ),
        compiler_params=pltpu.CompilerParams(vmem_limit_bytes=48 * 2**20),
        name="attention",
    )(tile_coords, extents, q, k, v, before, before, after, after, d_attn, so,
      log_sum[0][:, None, :])

    cut_a, cut_b = CUT, HALF - CUT
    weight_grad, from_next, from_prev = pl.pallas_call(
        scatter_kernel,
        out_shape=(jax.ShapeDtypeStruct((PAD, D), F32), pair, pair),
        in_specs=[vmem_spec(), any_spec(), any_spec()],
        out_specs=(vmem_spec(), any_spec(), any_spec()),
        scratch_shapes=[
            pltpu.VMEM((3, 4, BLK, cut_a), BF16),
            pltpu.VMEM((4, BLK, cut_a), BF16),
            pltpu.VMEM((3, 4, BLK, cut_b), BF16),
            pltpu.VMEM((4, BLK, cut_b), BF16),
            pltpu.VMEM((3, BLK, cut_a), BF16),
            pltpu.VMEM((3, BLK, cut_b), BF16),
            pltpu.VMEM((8, PAD, HALF), BF16),
            pltpu.VMEM((8, PAD, HALF), BF16),
            dma((2, 3)), dma((2, 3)), dma((2, 3)), dma((2, 3)), dma((7,)), dma((8,)),
            dma((2,)), dma((2,)),
        ],
        compiler_params=pltpu.CompilerParams(
            collective_id=1, has_side_effects=True, vmem_limit_bytes=48 * 2**20),
        name="scatter",
    )(wgrad.reshape(4, 4, BLK, HALF), to_prev, to_next)
    position = lax.axis_index("ctx")
    lower, upper = position > 0, position < 15

    def combine(own, i):
        total = own + jnp.where(upper, from_next[i].astype(F32), 0.0)
        total = total + jnp.where(lower, from_prev[i].astype(F32), 0.0)
        return total.astype(BF16)[None]

    return dq[None], combine(dk, 0), combine(dv, 1), weight_grad[:ROWS]


def solution(mesh):
    return jax.shard_map(
        shards,
        mesh=mesh,
        in_specs=(
            P("dp", "ctx", None),
            P("dp", "ctx", None),
            P("dp", "ctx", None),
            P("dp", "ctx", None),
            P("dp", None, "ctx"),
            P("dp", "ctx", None),
            P(("dp", "ctx"), None),
            P(),
            P(),
        ),
        out_specs=(
            P("dp", "ctx", None),
            P("dp", "ctx", None),
            P("dp", "ctx", None),
            P(("dp", "ctx"), None),
        ),
        check_vma=False,
    )
```

time: 1290 us -> 221 us (0.17)
  blocking collectives: 353 us -> 0 us
  local copies, waits for them, and re-layouts: 310 us -> 7.14 us
  waiting for transfers between devices: 229 us -> 0 us
  Pallas kernels: 0 us -> 206 us
  starting transfers between devices: 148 us -> 0 us
  matrix products: 137 us -> 0 us
  other arithmetic: 58.6 us -> 5.63 us
  loops' own time: 32.3 us -> 0 us
  between operations: 15 us -> 0.7 us
    unnamed x1 -> x0, blocking collectives: 353 us -> none
    pallas_call x0 -> x3, Pallas kernels: none -> 206 us  [the longest x1 105 us: shards(): pl.pallas_call(gather_kernel, out_shape=(pair, pair, jax.ShapeDtypeStruct...]
    all_gather x1 -> x0, waiting for transfers between devices: 139 us -> none  [shards(): lax.all_gather(out_weight, ('dp', 'ctx'), axis=0, tiled=True)]
    dot_general x62 -> x0, matrix products: 137 us -> none  [the longest x12 28.7 us: per_head(): jnp.einsum('bij,bid->bjd', d_scores, q_head, preferred_element_type=jnp.f...]
    unnamed x32 -> x0, starting transfers between devices: 133 us -> none
    unnamed x80 -> x21, local copies, waits for them, and re-layouts: 111 us -> 6.24 us
    slice x12 -> x0, local copies, waits for them, and re-layouts: 95.7 us -> none  [per_head(): v_near = head_slice(widened[1], head)]
    dynamic_update_slice x48 -> x0, local copies, waits for them, and re-layouts: 63.8 us -> none  [shards(): query_parts, key_terms, value_terms = lax.map(per_head, head_ids)]
  transfers between devices with their start and end apart: 37 -> 0, of which waited for: 18 -> 0; matrix products, arithmetic and copies ran while one was open for 36% -> 0% of each run, Pallas kernels for 0% -> 0%
where the time goes in v1:
time: 221 us; the launch traced here: 219 us
  Pallas kernels  206 us (93%)
  local copies, waits for them, and re-layouts  7.14 us (3%)
  other arithmetic  5.63 us (3%)
    pallas_call x1, Pallas kernels, shards(): pl.pallas_call(gather_kernel, out_shape=(pair, pair, jax.ShapeDtypeStruct...  105 us
    pallas_call x1, Pallas kernels, shards(): pl.pallas_call(scatter_kernel, out_shape=(jax.ShapeDtypeStruct((PAD, D),...  71.9 us
    pallas_call x1, Pallas kernels, shards(): pl.pallas_call(attention_kernel, out_shape=(own16, own32, own32, pair, pa...  29.5 us
    unnamed x21, local copies, waits for them, and re-layouts  6.24 us
    broadcast_in_dim x1, other arithmetic, combine(): return total.astype(BF16)[None]  5.63 us

profile of v1, /device:TPU:4, one launch (start us, length us, event | category | flops | bytes accessed | tf_op | source)
XLA Modules:
  0.0 219.4 jit_solution(8621037632188703619)
XLA Ops:
  0.6 0.9 pad.4.strip
  1.5 0.0 copy-start
  1.6 1.4 copy-done
  3.0 0.0 copy-start.2
  3.0 1.4 copy-done.2
  4.4 0.0 copy-start.7
  4.4 0.0 copy-start.8
  4.4 0.0 copy-start.1
  4.4 0.0 copy-start.3
  4.4 0.0 copy-start.6
  4.4 104.5 %gather.1 = (bf16[2,512,1536]{2,1,0:T(8,128)(2,1)}, bf16[2,512,1536]{2,1,0:T(8,128)(2,1)}, bf16[512,1536]{1,0:T(8,128)(2,1)S(1)}, bf16[1536,1536]{1,0:T(8,128)(2,1)}) custom-call(bf16[16,3072]{1,0:T(8,128)(2,1)S(1)} %pad.4.strip, bf16[512,1536]{1,0:T(8,128)(2,1)S(1)} %bitcast.37, bf16[512,1536]{1,0:T(8,128)(2,1)S(1)} %bitcast.39, ...), custom_call_target="tpu_custom_call" | custom-call | tf_op jit(solution)/shard_map/gather/pallas_call | solution.py:486
  108.9 0.0 copy-start.5
  108.9 1.1 copy-done.5
  110.0 0.0 copy-done.7
  110.0 0.1 copy.13.coords
  110.1 0.0 copy-done.8
  110.1 0.1 copy.14.extents
  110.2 0.0 copy-done.1
  110.2 0.0 copy-done.3
  110.2 0.0 copy-done.6
  110.2 0.0 copy-start.4
  110.3 1.4 copy-done.4
  111.7 29.5 %attention.1 = (bf16[512,1536]{1,0:T(8,128)(2,1)}, f32[512,1536]{1,0:T(8,128)}, f32[512,1536]{1,0:T(8,128)}, bf16[2,512,1536]{2,1,0:T(8,128)(2,1)}, bf16[2,512,1536]{2,1,0:T(8,128)(2,1)}) custom-call(s32[64,3]{1,0:T(8,128)S(1)} %copy.13.coords, s32[12,3]{1,0:T(8,128)S(1)} %copy.14.extents, bf16[512,1536]{1,0:T(8,128)(2,1)S(1)} %bitcast.41, ...), custom_call_target="tpu_custom_call" | custom-call | tf_op jit(solution)/shard_map/attention/pallas_call | solution.py:514
  141.2 71.9 %scatter.1 = (f32[16,3072]{1,0:T(8,128)S(1)}, bf16[2,512,1536]{2,1,0:T(8,128)(2,1)S(1)}, bf16[2,512,1536]{2,1,0:T(8,128)(2,1)}) custom-call(bf16[4,4,96,1536]{3,2,1,0:T(8,128)(2,1)} %bitcast.46, bf16[2,512,1536]{2,1,0:T(8,128)(2,1)} %get-tuple-element.22.to_prev, bf16[2,512,1536]{2,1,0:T(8,128)(2,1)} %get-tuple-element.23.to_next), custom_call_target="tpu_custom_call" | custom-call | tf_op jit(solution)/shard_map/scatter/pallas_call | solution.py:540
  213.1 5.6 %fusion.3 = (bf16[1,512,1536]{2,1,0:T(8,128)(2,1)}, bf16[1,512,1536]{2,1,0:T(8,128)(2,1)}) fusion(f32[512,1536]{1,0:T(8,128)} %get-tuple-element.26, bf16[2,512,1536]{2,1,0:T(8,128)(2,1)} %get-tuple-element.25, bf16[2,512,1536]{2,1,0:T(8,128)(2,1)S(1)} %get-tuple-element.24, pred[]{:T(512)S(6)} %gt.3, pred[]{:T(512)S(6)} %lt.3, f32[512,1536]{1,0:T(8,128)} %get-tuple-element.20), kind=kLoop, calls=%fused_computation.7 | loop fusion | flops 11010048 | bytes 15728642 | tf_op jit(solution)/shard_map/broadcast_in_dim | solution.py:567
  218.7 0.7 copy.16
Async XLA Ops:
  1.5 1.4 copy-start
  3.0 1.4 copy-start.2
  4.4 105.7 %copy-start.7 = (s32[64,3]{0,1:T(4,128)S(1)}, s32[64,3]{0,1:T(4,128)}, u32[]{:S(2)}) copy-start(s32[64,3]{0,1:T(4,128)} %param.16) | copy-start | bytes 2308
  4.4 105.8 %copy-start.8 = (s32[12,3]{0,1:T(4,128)S(1)}, s32[12,3]{0,1:T(4,128)}, u32[]{:S(2)}) copy-start(s32[12,3]{0,1:T(4,128)} %param.17) | copy-start | bytes 436
  4.4 105.9 %copy-start.1 = (bf16[1,512,1536]{2,1,0:T(8,128)(2,1)S(1)}, bf16[1,512,1536]{2,1,0:T(8,128)(2,1)}, u32[]{:S(2)}) copy-start(bf16[1,512,1536]{2,1,0:T(8,128)(2,1)} %param.10) | copy-start | bytes 4718596
  4.4 105.9 %copy-start.3 = (bf16[1,512,1536]{2,1,0:T(8,128)(2,1)S(1)}, bf16[1,512,1536]{2,1,0:T(8,128)(2,1)}, u32[]{:S(2)}) copy-start(bf16[1,512,1536]{2,1,0:T(8,128)(2,1)} %param.11) | copy-start | bytes 4718596
  4.4 105.9 %copy-start.6 = (f32[1,12,512]{2,0,1:T(1,128)S(1)}, f32[1,12,512]{2,0,1:T(1,128)}, u32[]{:S(2)}) copy-start(f32[1,12,512]{2,0,1:T(1,128)} %param.13) | copy-start | bytes 73732
  108.9 1.1 copy-start.5
  110.2 1.4 copy-start.4

commit v2 on v1

--- a/solution.py
+++ b/solution.py
@@ -18,8 +18,11 @@
 ROWS = 12
 PAD = 16
 BLK = 8 * ROWS
-CUT = 1024
+CUT = 1152
 PARTS = ((0, CUT), (CUT, HALF))
+SUM_CUT = 768
+SUM_PARTS = ((0, SUM_CUT), (SUM_CUT, HALF))
+SUB = SUM_CUT // 2
 STEPS = (1, 3, 2)
 MESH = pl.DeviceIdType.MESH
 F32 = jnp.float32
@@ -50,8 +53,6 @@
 
 
 def greet(z, x, y, c):
-    ctx = lax.axis_index("ctx")
-    dp = lax.axis_index("dp")
     barrier = pltpu.get_barrier_semaphore()
 
     def tell(target):
@@ -64,6 +65,8 @@
     for step in STEPS:
         tell(device(z, (x + step) % 4, y, c))
         tell(device((z + step) % 4, x, y, c))
+
+    ctx, dp = lax.axis_index("ctx"), lax.axis_index("dp")
 
     @pl.when(ctx == 7)
     def _():
@@ -122,16 +125,22 @@
 
 
 def gather_kernel(
-    strip, keys, vals, so, og,
-    before, after, d_attn, wgrad,
-    strips, full, so_sib, og_sib,
-    strip_send, strip_recv, near_send, far_send, ag_recv, sib_send, sib_recv,
-    ex_send, ex_recv, halo_send, halo_recv,
+    strip, keys, vals, so_hbm, og_hbm,
+    before, after, d_attn_out, keep_a_out, send_a_out, keep_b_out, send_b_out,
+    strips, full, so, og, so_sib, og_sib, turn, d_attn, keep_a, send_a, keep_b, send_b,
+    strip_send, strip_recv, near_send, far_send, pass_send, ag_recv, late_recv, sib_send, sib_recv,
+    ex_send, ex_recv, halo_send, halo_recv, load_sem, store_sem,
 ):
     z, x, y, c = place()
     sib = device(z, x, y, 1 - c)
     me = block_of(z, x)
     slot = y * 2 + c
+    loads = [pltpu.make_async_copy(so_hbm, so, load_sem.at[0]),
+             pltpu.make_async_copy(og_hbm, og, load_sem.at[1])]
+    for copy in loads:
+        copy.start()
+    strips[slot, 0:ROWS] = strip[...]
+    strips[slot, ROWS:PAD] = jnp.zeros((PAD - ROWS, D), BF16)
     greet(z, x, y, c)
 
     pending = []
@@ -139,28 +148,24 @@
     for dy in range(4):
         for dc in range(2):
             if dy or dc:
-                copy = remote(strip, strips.at[slot], strip_send.at[number], strip_recv.at[slot],
-                              device(z, x, (y + dy) % 4, (c + dc) % 2))
+                copy = remote(strips.at[slot], strips.at[slot], strip_send.at[number],
+                              strip_recv.at[slot], device(z, x, (y + dy) % 4, (c + dc) % 2))
                 copy.start()
                 pending.append(copy)
                 number += 1
     other = pl.ds(pl.multiple_of((1 - c) * HALF, HALF), HALF)
     exchange = [
-        remote(so, so_sib, ex_send.at[0], ex_recv.at[0], sib),
-        remote(og.at[:, other], og_sib, ex_send.at[1], ex_recv.at[1], sib),
+        remote(so_hbm, so_sib, ex_send.at[0], ex_recv.at[0], sib),
+        remote(og_hbm.at[:, other], og_sib, ex_send.at[1], ex_recv.at[1], sib),
     ]
     for copy in exchange:
         copy.start()
-    halos = halo_copies(
-        [(keys, before.at[0]), (vals, before.at[1]), (keys, after.at[0]), (vals, after.at[1])],
-        halo_send, halo_recv)
-    halo_start(halos)
-    strips[slot] = strip[...]
     for dy in range(4):
         for dc in range(2):
             if dy or dc:
                 src = ((y + dy) % 4) * 2 + (c + dc) % 2
-                remote(strip, strips.at[src], strip_send.at[0], strip_recv.at[src], sib).wait_recv()
+                remote(strips.at[src], strips.at[src], strip_send.at[0], strip_recv.at[src],
+                       sib).wait_recv()
     row = lax.broadcasted_iota(jnp.int32, (BLK, 8 * PAD), 0)
     col = lax.broadcasted_iota(jnp.int32, (BLK, 8 * PAD), 1)
     pick = jnp.where(col == (row // ROWS) * PAD + row % ROWS, 1.0, 0.0).astype(BF16)
@@ -191,11 +196,29 @@
             pending.append(copy)
 
     def onward(part, block, j):
-        for i, step in enumerate(STEPS):
+        for i, step in enumerate((1, 3)):
             copy = remote(piece(c, block, part), piece(c, block, part), far_send.at[part, j, i],
                           ag_recv.at[part, block], along(part, False, step))
             copy.start()
             pending.append(copy)
+
+    def half_piece(block, part, upper):
+        low, high = PARTS[part]
+        return full.at[c, block, (BLK // 2 if upper else 0):(BLK if upper else BLK // 2), low:high]
+
+    def pass_on(part, block, j, step):
+        upper = step == 1
+        copy = remote(half_piece(block, part, upper), half_piece(block, part, upper),
+                      pass_send.at[part, j, int(upper)],
+                      (late_recv if upper else ag_recv).at[part, block],
+                      along(part, False, 4 - step))
+        copy.start()
+        pending.append(copy)
+
+    def arrived_late(part, block):
+        for upper, sem in ((False, ag_recv), (True, late_recv)):
+            remote(half_piece(block, part, upper), half_piece(block, part, upper),
+                   near_send.at[part, 0], sem.at[part, block], sib).wait_recv()
 
     def to_sibling(part, block):
         copy = remote(piece(c, block, part), piece(c, block, part), sib_send.at[part, block],
@@ -210,16 +233,43 @@
     for part in range(2):
         onward(part, me, 0)
 
+    halos = halo_copies(
+        [(keys, before.at[0]), (vals, before.at[1]), (keys, after.at[0]), (vals, after.at[1])],
+        halo_send, halo_recv)
+    halo_start(halos)
     for copy in exchange:
         copy.wait_recv()
-    mine = pl.ds(pl.multiple_of(c * HALF, HALF), HALF)
-
-    def wgrad_rows(i, carry):
-        rows = pl.ds(pl.multiple_of(i * 256, 256), 256)
-        total = lax.dot_general(so[:, rows], og[:, mine], TN, preferred_element_type=F32)
-        total += lax.dot_general(so_sib[:, rows], og_sib[...], TN, preferred_element_type=F32)
-        wgrad[rows, :] = total.astype(BF16)
-        return carry
+    for copy in loads:
+        copy.wait()
+    def wgrad_group(group, j):
+        rows = pl.ds(pl.multiple_of(group * 4 * BLK, 4 * BLK), 4 * BLK)
+        for low, high in SUM_PARTS:
+            cols = pl.ds(pl.multiple_of(c * HALF + low, 128), high - low)
+            total = lax.dot_general(so[:, rows], og[:, cols], TN, preferred_element_type=F32)
+            total += lax.dot_general(so_sib[:, rows], og_sib[:, low:high], TN,
+                                     preferred_element_type=F32)
+            total = total.astype(BF16).reshape(4, BLK, high - low)
+            if low:
+                turn[...] = total
+            elif j == 0:
+                keep_a[0] = total
+            elif j == 2:
+                send_a[0] = total
+            else:
+                first, other = (keep_a, send_a) if j == 1 else (send_a, keep_a)
+                first[1, :, :, :SUB] = total[:, :, :SUB]
+                other[1, :, :, SUB:] = total[:, :, SUB:]
+        for k in range(4):
+            tx = (x + k) % 4
+            total = turn[(tx % 2) * 2 + tx // 2]
+            if k == 0:
+                keep_b[0, group] = total
+            elif k == 2:
+                send_b[0, group] = total
+            else:
+                first, other = (keep_b, send_b) if k == 1 else (send_b, keep_b)
+                first[1, group, :, :SUB] = total[:, :SUB]
+                other[1, group, :, SUB:] = total[:, SUB:]
 
     for j, step in enumerate(STEPS):
         for part in range(2):
@@ -227,16 +277,27 @@
             arrived(part, block)
             onward(part, block, j + 1)
             to_sibling(part, block)
-    lax.fori_loop(0, HD // 256, wgrad_rows, 0)
+    for j in range(4):
+        wgrad_group((z + j) % 4, j)
+    stores = []
+    for j, (src, dst) in enumerate(((keep_a, keep_a_out), (send_a, send_a_out),
+                                    (keep_b, keep_b_out), (send_b, send_b_out))):
+        stores.append(pltpu.make_async_copy(src, dst, store_sem.at[j]))
+        stores[-1].start()
 
     for step in STEPS:
-        for inner in (0,) + STEPS:
-            block = block_of((z + step) % 4, (x + inner) % 4)
-            arrived(0, block)
-            to_sibling(0, block)
-            block = block_of((z + inner) % 4, (x + step) % 4)
-            arrived(1, block)
-            to_sibling(1, block)
+        for j, inner in enumerate((0,) + STEPS):
+            for part in range(2):
+                if part == 0:
+                    block = block_of((z + step) % 4, (x + inner) % 4)
+                else:
+                    block = block_of((z + inner) % 4, (x + step) % 4)
+                if step == 2:
+                    arrived_late(part, block)
+                else:
+                    arrived(part, block)
+                    pass_on(part, block, j, step)
+                to_sibling(part, block)
 
     for step in (0,) + STEPS:
         group = (z + step) % 4
@@ -260,7 +321,12 @@
             return carry
 
         lax.fori_loop(0, TOK // 256, project, 0)
+        stores.append(pltpu.make_async_copy(d_attn.at[:, feats], d_attn_out.at[:, feats],
+                                            store_sem.at[4 + step]))
+        stores[-1].start()
     halo_wait(halos)
+    for copy in stores:
+        copy.wait()
     for copy in exchange:
         copy.wait_send()
     for copy in pending:
@@ -268,41 +334,45 @@
 
 
 def scatter_kernel(
-    wgrad, to_prev, to_next,
+    to_prev, to_next, keep_a_in, got_a_in, keep_b_in, got_b_in,
     out, from_next, from_prev,
-    got_a, sum_a, got_b, sum_b, got_a2, got_b2, packed, last,
-    first_send, first_recv, second_send, second_recv, last_send, last_recv, halo_send, halo_recv,
+    keep_a, got_a, keep_b, got_b, pass_a, pass_b, more_a, more_b,
+    sum_a, sum_b, got_a2, got_b2, packed, last,
+    first_send, first_recv, second_send, second_recv, last_send, last_recv,
+    halo_send, halo_recv, load_sem,
 ):
     z, x, y, c = place()
     slot = y * 2 + c
+    (low_a, high_a), (low_b, high_b) = SUM_PARTS
+    loads = []
+    for j, (src, dst) in enumerate(((keep_a_in, keep_a), (got_a_in, got_a),
+                                    (keep_b_in, keep_b), (got_b_in, got_b))):
+        loads.append(pltpu.make_async_copy(src, dst, load_sem.at[j]))
+        loads[-1].start()
     greet(z, x, y, c)
-    (a0, a1), (b0, b1) = PARTS
-    pending = []
-    for i, step in enumerate(STEPS):
-        tz, tx = (z + step) % 4, (x + step) % 4
-        for part, src, dst, target in (
-            (0, wgrad.at[tz, :, :, a0:a1], got_a.at[i], device(tz, x, y, c)),
-            (1, wgrad.at[:, (tx % 2) * 2 + tx // 2, :, b0:b1], got_b.at[i], device(z, tx, y, c)),
-        ):
-            copy = remote(src, dst, first_send.at[part, i], first_recv.at[part, i], target)
+    halos = halo_copies([(to_next, from_prev), (to_prev, from_next)], halo_send, halo_recv)
+    for copy in loads:
+        copy.wait()
+    first = []
+    for part, (keep, got, ready, more) in enumerate(
+            ((keep_a, got_a, pass_a, more_a), (keep_b, got_b, pass_b, more_b))):
+        for j in range(4):
+            ready[j] = (keep[1, j].astype(F32) + got[1, j].astype(F32)).astype(BF16)
+        for i, (cols, step) in enumerate(((slice(0, SUB), 1), (slice(SUB, 2 * SUB), 3))):
+            target = device(z, (x + step) % 4, y, c) if part else device((z + step) % 4, x, y, c)
+            copy = remote(ready.at[:, :, cols], more.at[:, :, cols], first_send.at[part, i],
+                          first_recv.at[part, i], target)
             copy.start()
-            pending.append(copy)
-    halos = halo_copies(
-        [(to_next, from_prev), (to_prev, from_next)], halo_send, halo_recv)
+            first.append(copy)
     halo_start(halos)
-    for i in range(3):
-        pending[2 * i].wait_recv()
-        pending[2 * i + 1].wait_recv()
+    for copy in first:
+        copy.wait_recv()
+    for keep, got, more, total_ref in (
+            (keep_a, got_a, more_a, sum_a), (keep_b, got_b, more_b, sum_b)):
+        for j in range(4):
+            total = keep[0, j].astype(F32) + got[0, j].astype(F32) + more[j].astype(F32)
+            total_ref[j] = total.astype(BF16)
     xs = (x % 2) * 2 + x // 2
-    for j in range(4):
-        total = wgrad[z, j, :, a0:a1].astype(F32)
-        for i in range(3):
-            total += got_a[i, j].astype(F32)
-        sum_a[j] = total.astype(BF16)
-        total = wgrad[j, xs, :, b0:b1].astype(F32)
-        for i in range(3):
-            total += got_b[i, j].astype(F32)
-        sum_b[j] = total.astype(BF16)
     second = []
     for i, step in enumerate(STEPS):
         tz, tx = (z + step) % 4, (x + step) % 4
@@ -324,10 +394,10 @@
     for i in range(3):
         total_a += got_a2[i].astype(F32)
         total_b += got_b2[i].astype(F32)
-    packed[:, :, a0:a1] = jnp.dot(spread, total_a.astype(BF16), preferred_element_type=F32).astype(
-        BF16).reshape(8, PAD, a1 - a0)
-    packed[:, :, b0:b1] = jnp.dot(spread, total_b.astype(BF16), preferred_element_type=F32).astype(
-        BF16).reshape(8, PAD, b1 - b0)
+    packed[:, :, low_a:high_a] = jnp.dot(spread, total_a.astype(BF16), preferred_element_type=F32).astype(
+        BF16).reshape(8, PAD, high_a - low_a)
+    packed[:, :, low_b:high_b] = jnp.dot(spread, total_b.astype(BF16), preferred_element_type=F32).astype(
+        BF16).reshape(8, PAD, high_b - low_b)
     number = 0
     third = []
     for dy in range(4):
@@ -350,9 +420,9 @@
         total = last[h].astype(F32)
         for i in range(1, 4):
             total += last[2 * i + h].astype(F32)
-        out[:, h * HALF:(h + 1) * HALF] = total * (1.0 / 256.0)
+        out[:, h * HALF:(h + 1) * HALF] = total[:ROWS] * (1.0 / 256.0)
     halo_wait(halos)
-    for copy in pending + second + third:
+    for copy in first + second + third:
         copy.wait_send()
 
 
@@ -468,58 +538,87 @@
         dq_ref[rows(1, s), :] = (dqt_s[:, s * TILE:(s + 1) * TILE].T * scale).astype(BF16)
 
 
+def combine_kernel(dk, dv, ahead, behind, key_out, value_out):
+    frame = lax.axis_index("ctx")
+    for i, (own, out) in enumerate(((dk, key_out), (dv, value_out))):
+        total = own[...] + jnp.where(frame < 15, ahead[i].astype(F32), 0.0)
+        total += jnp.where(frame > 0, behind[i].astype(F32), 0.0)
+        out[...] = total.astype(BF16)
+
+
 def any_spec():
     return pl.BlockSpec(memory_space=pl.ANY)
 
 
 def vmem_spec():
     return pl.BlockSpec(memory_space=pltpu.VMEM)
+
+
+def along_x(value, step):
+    pairs = []
+    for dp in range(8):
+        for ctx in range(16):
+            x = (ctx // 8) * 2 + dp % 2
+            tx = (x + step) % 4
+            pairs.append((dp * 16 + ctx, ((dp // 2) * 2 + tx % 2) * 16 + (tx // 2) * 8 + ctx % 8))
+    return lax.ppermute(value, ("dp", "ctx"), pairs)
+
+
+def along_z(value, step):
+    return lax.ppermute(value, "dp", [(i, (i + 2 * step) % 8) for i in range(8)])
 
 
 def shards(
     queries, key_rows, values, saved_out, log_sum, out_grad, out_weight, tile_coords, extents
 ):
     q, k, v, so, og = (a[0] for a in (queries, key_rows, values, saved_out, out_grad))
-    strip = jnp.pad(out_weight, ((0, PAD - ROWS), (0, 0)))
+    col = pl.BlockSpec((TOK, HEAD), lambda h, *_: (0, h))
+    pair = jax.ShapeDtypeStruct((2, TOK, HD), BF16)
     dma = pltpu.SemaphoreType.DMA
-    pair = jax.ShapeDtypeStruct((2, TOK, HD), BF16)
-    before, after, d_attn, wgrad = pl.pallas_call(
+    moving = jax.ShapeDtypeStruct((2, 4, BLK, SUM_CUT), BF16)
+    before, after, d_attn, keep_a, send_a, keep_b, send_b = pl.pallas_call(
         gather_kernel,
-        out_shape=(pair, pair, jax.ShapeDtypeStruct((TOK, HD), BF16),
-                   jax.ShapeDtypeStruct((HD, HALF), BF16)),
-        in_specs=[vmem_spec(), any_spec(), any_spec(), vmem_spec(), vmem_spec()],
-        out_specs=(any_spec(), any_spec(), vmem_spec(), vmem_spec()),
+        out_shape=(pair, pair, jax.ShapeDtypeStruct((TOK, HD), BF16)) + (moving,) * 4,
+        in_specs=[vmem_spec()] + [any_spec()] * 4,
+        out_specs=(any_spec(),) * 7,
         scratch_shapes=[
             pltpu.VMEM((8, PAD, D), BF16),
             pltpu.VMEM((2, 16, BLK, HALF), BF16),
             pltpu.VMEM((TOK, HD), BF16),
+            pltpu.VMEM((TOK, D), BF16),
+            pltpu.VMEM((TOK, HD), BF16),
             pltpu.VMEM((TOK, HALF), BF16),
-            dma((7,)), dma((8,)), dma((2, 3)), dma((2, 4, 3)), dma((2, 16)), dma((2, 16)),
-            dma((2, 16)), dma((2,)), dma((2,)), dma((4,)), dma((4,)),
+            pltpu.VMEM((4, BLK, SUM_CUT), BF16),
+            pltpu.VMEM((TOK, HD), BF16),
+        ] + [pltpu.VMEM((2, 4, BLK, SUM_CUT), BF16)] * 4 + [
+            dma((7,)), dma((8,)), dma((2, 3)), dma((2, 4, 2)), dma((2, 4, 2)), dma((2, 16)),
+            dma((2, 16)), dma((2, 16)), dma((2, 16)), dma((2,)), dma((2,)), dma((4,)), dma((4,)),
+            dma((2,)), dma((8,)),
         ],
         compiler_params=pltpu.CompilerParams(
-            collective_id=0, has_side_effects=True, vmem_limit_bytes=48 * 2**20),
+            collective_id=0, has_side_effects=True, vmem_limit_bytes=56 * 2**20),
+        cost_estimate=pl.CostEstimate(
+            flops=10**10, bytes_accessed=20 * 10**6, transcendentals=0),
         name="gather",
-    )(strip, k, v, so, og)
-
-    def col():
-        return pl.BlockSpec((TOK, HEAD), lambda h, *_: (0, h))
-
-    def pair_col(i):
-        return pl.BlockSpec((None, TOK, HEAD), lambda h, *_: (i, 0, h))
-
-    both = pl.BlockSpec((2, TOK, HEAD), lambda h, *_: (0, 0, h))
+    )(out_weight, k, v, so, og)
+    got_a, got_b = along_z(send_a, 2), along_x(send_b, 2)
+
     own32 = jax.ShapeDtypeStruct((TOK, HD), F32)
     own16 = jax.ShapeDtypeStruct((TOK, HD), BF16)
+    row = pl.BlockSpec((None, 1, TOK), lambda h, *_: (h, 0, 0))
+
+    def side(i):
+        return pl.BlockSpec((None, TOK, HEAD), lambda h, *_, i=i: (i, 0, h))
+
+    sides = pl.BlockSpec((2, TOK, HEAD), lambda h, *_: (0, 0, h))
     dq, dk, dv, to_prev, to_next = pl.pallas_call(
         attention_kernel,
         out_shape=(own16, own32, own32, pair, pair),
         grid_spec=pltpu.PrefetchScalarGridSpec(
             num_scalar_prefetch=2,
             grid=(H,),
-            in_specs=[col(), col(), col(), pair_col(0), pair_col(1), pair_col(0), pair_col(1),
-                      col(), col(), pl.BlockSpec((None, 1, TOK), lambda h, *_: (h, 0, 0))],
-            out_specs=(col(),) * 3 + (both,) * 2,
+            in_specs=[col] * 3 + [side(0), side(1)] * 2 + [col] * 2 + [row],
+            out_specs=(col,) * 3 + (sides,) * 2,
             scratch_shapes=[
                 pltpu.SMEM((2, 3, 4), jnp.int32),
                 pltpu.VMEM((TOK, HEAD), BF16),
@@ -532,41 +631,45 @@
             ],
         ),
         compiler_params=pltpu.CompilerParams(vmem_limit_bytes=48 * 2**20),
+        cost_estimate=pl.CostEstimate(
+            flops=12 * 10**9, bytes_accessed=30 * 10**6, transcendentals=10**7),
         name="attention",
     )(tile_coords, extents, q, k, v, before, before, after, after, d_attn, so,
       log_sum[0][:, None, :])
 
-    cut_a, cut_b = CUT, HALF - CUT
     weight_grad, from_next, from_prev = pl.pallas_call(
         scatter_kernel,
-        out_shape=(jax.ShapeDtypeStruct((PAD, D), F32), pair, pair),
-        in_specs=[vmem_spec(), any_spec(), any_spec()],
+        out_shape=(jax.ShapeDtypeStruct((ROWS, D), F32), pair, pair),
+        in_specs=[any_spec()] * 6,
         out_specs=(vmem_spec(), any_spec(), any_spec()),
-        scratch_shapes=[
-            pltpu.VMEM((3, 4, BLK, cut_a), BF16),
-            pltpu.VMEM((4, BLK, cut_a), BF16),
-            pltpu.VMEM((3, 4, BLK, cut_b), BF16),
-            pltpu.VMEM((4, BLK, cut_b), BF16),
-            pltpu.VMEM((3, BLK, cut_a), BF16),
-            pltpu.VMEM((3, BLK, cut_b), BF16),
+        scratch_shapes=[pltpu.VMEM((2, 4, BLK, SUM_CUT), BF16)] * 4
+        + [pltpu.VMEM((4, BLK, SUM_CUT), BF16)] * 6
+        + [pltpu.VMEM((3, BLK, SUM_CUT), BF16)] * 2 + [
             pltpu.VMEM((8, PAD, HALF), BF16),
             pltpu.VMEM((8, PAD, HALF), BF16),
-            dma((2, 3)), dma((2, 3)), dma((2, 3)), dma((2, 3)), dma((7,)), dma((8,)),
-            dma((2,)), dma((2,)),
+            dma((2, 2)), dma((2, 2)), dma((2, 3)), dma((2, 3)), dma((7,)), dma((8,)),
+            dma((2,)), dma((2,)), dma((4,)),
         ],
         compiler_params=pltpu.CompilerParams(
             collective_id=1, has_side_effects=True, vmem_limit_bytes=48 * 2**20),
+        cost_estimate=pl.CostEstimate(
+            flops=10**10, bytes_accessed=20 * 10**6, transcendentals=0),
         name="scatter",
-    )(wgrad.reshape(4, 4, BLK, HALF), to_prev, to_next)
-    position = lax.axis_index("ctx")
-    lower, upper = position > 0, position < 15
-
-    def combine(own, i):
-        total = own + jnp.where(upper, from_next[i].astype(F32), 0.0)
-        total = total + jnp.where(lower, from_prev[i].astype(F32), 0.0)
-        return total.astype(BF16)[None]
-
-    return dq[None], combine(dk, 0), combine(dv, 1), weight_grad[:ROWS]
+    )(to_prev, to_next, keep_a, got_a, keep_b, got_b)
+
+    wide = HD // 4
+    whole = pl.BlockSpec((TOK, wide), lambda i: (0, i))
+    halo = pl.BlockSpec((2, TOK, wide), lambda i: (0, 0, i))
+    key_grad, value_grad = pl.pallas_call(
+        combine_kernel,
+        out_shape=(own16, own16),
+        grid=(4,),
+        in_specs=[whole, whole, halo, halo],
+        out_specs=(whole, whole),
+        compiler_params=pltpu.CompilerParams(vmem_limit_bytes=48 * 2**20),
+        name="combine",
+    )(dk, dv, from_next, from_prev)
+    return dq[None], key_grad[None], value_grad[None], weight_grad
 
 
 def solution(mesh):

time: 221 us -> 186 us (0.84)
  Pallas kernels: 206 us -> 180 us
  other arithmetic: 5.63 us -> 0 us
  local copies, waits for them, and re-layouts: 7.14 us -> 2.3 us
    pallas_call x1, Pallas kernels: 105 us -> 89.5 us  [shards(): pl.pallas_call(gather_kernel, out_shape=(pair, pair, jax.ShapeDtypeStruct...]
    pallas_call x1 -> x2, Pallas kernels: 71.9 us -> 63.3 us  [the longest x1 57.3 us: shards(): pl.pallas_call(scatter_kernel, out_shape=(jax.ShapeDtypeStruct((ROWS, D),...]
    broadcast_in_dim x1 -> x0, other arithmetic: 5.63 us -> none  [combine(): return total.astype(BF16)[None]]
    unnamed x21, local copies, waits for them, and re-layouts: 6.24 us -> 2.3 us
    pallas_call x1, Pallas kernels: 29.5 us -> 27 us  [shards(): pl.pallas_call(attention_kernel, out_shape=(own16, own32, own32, pair, pa...]
  transfers between devices with their start and end apart: 0 -> 2, of which waited for: 0 -> 0; matrix products, arithmetic and copies ran while one was open for 0% -> 0% of each run, Pallas kernels for 0% -> 15%
where the time goes in v2:
time: 186 us; the launch traced here: 184 us
  Pallas kernels  180 us (97%)
  local copies, waits for them, and re-layouts  2.3 us (1%)
    pallas_call x1, Pallas kernels, shards(): pl.pallas_call(gather_kernel, out_shape=(pair, pair, jax.ShapeDtypeStruct...  89.5 us
    pallas_call x1, Pallas kernels, shards(): pl.pallas_call(scatter_kernel, out_shape=(jax.ShapeDtypeStruct((ROWS, D),...  57.3 us
    pallas_call x1, Pallas kernels, shards(): pl.pallas_call(attention_kernel, out_shape=(own16, own32, own32, pair, pa...  27 us
    pallas_call x1, Pallas kernels, shards(): pl.pallas_call(combine_kernel, out_shape=(own16, own16), grid=(4,), in_sp...  6.03 us
  transfers between devices with their start and end apart: 2, of which 0 were waited for; matrix products, arithmetic and copies ran while one was open for 0% of the time, Pallas kernels for 15%

profile of v2, /device:TPU:4, one launch (start us, length us, event | category | flops | bytes accessed | tf_op | source)
XLA Modules:
  0.0 184.0 jit_solution(17252760826458026618)
XLA Ops:
  0.6 0.0 copy-start.7
  0.6 0.0 copy-start.8
  0.7 0.0 copy-start.1
  0.7 0.0 copy-start.2
  0.7 0.0 copy-start.4
  0.7 89.5 %gather.1 = (bf16[2,512,1536]{2,1,0:T(8,128)(2,1)}, bf16[2,512,1536]{2,1,0:T(8,128)(2,1)}, bf16[512,1536]{1,0:T(8,128)(2,1)}, bf16[2,4,96,768]{3,2,1,0:T(8,128)(...) custom-call(bf16[12,3072]{1,0:T(8,128)(2,1)} %strip.1, ...), custom_call_target="tpu_custom_call" | custom-call | flops 10000000000 | bytes 20000000 | tf_op jit(solution)/shard_map/gather/pallas_call | solution.py:579
  90.2 1.1 collective-permute-start
  91.3 0.0 collective-permute-start.1
  91.3 0.0 copy-done.7
  91.3 0.1 copy.14.extents
  91.4 0.0 copy-done.8
  91.4 0.1 copy.13.coords
  91.5 0.0 copy-done.1
  91.5 0.0 copy-done.2
  91.5 0.0 copy-done.4
  91.5 0.0 copy-start.3
  91.5 1.4 copy-done.3
  92.9 0.0 copy-start.5
  92.9 0.0 copy-start.6
  92.9 27.0 %attention.1 = (bf16[512,1536]{1,0:T(8,128)(2,1)}, f32[512,1536]{1,0:T(8,128)}, f32[512,1536]{1,0:T(8,128)}, bf16[2,512,1536]{2,1,0:T(8,128)(2,1)}, bf16[2,512,1536]{2,1,0:T(8,128)(2,1)}) custom-call(s32[64,3]{1,0:T(8,128)S(1)} %copy.13.coords, s32[12,3]{1,0:T(8,128)S(1)} %copy.14.extents, bf16[512,1536]{1,0:T(8,128)(2,1)S(1)} %bitcast.9, ...), custom_call_target="tpu_custom_call" | custom-call | flops 12000000000 | bytes 30000000 | tf_op jit(solution)/shard_map/attention/pallas_call | solution.py:614
  119.9 0.0 collective-permute-done.got_a_in
  119.9 0.0 collective-permute-done.1.got_b_in
  120.0 0.0 copy-done.5
  120.0 0.0 copy-done.6
  120.0 0.0 copy-start
  120.0 57.3 %scatter.1 = (f32[12,3072]{1,0:T(8,128)S(1)}, bf16[2,512,1536]{2,1,0:T(8,128)(2,1)}, bf16[2,512,1536]{2,1,0:T(8,128)(2,1)}) custom-call(bf16[2,512,1536]{2,1,0:T(8,128)(2,1)} %get-tuple-element.27.to_prev, bf16[2,512,1536]{2,1,0:T(8,128)(2,1)} %get-tuple-element.28.to_next, bf16[2,4,96,768]{3,2,1,0:T(8,128)(2,1)S(1)} %copy-done.5, ...), custom_call_target="tpu_custom_call" | custom-call | flops 10000000000 | bytes 20000000 | tf_op jit(solution)/shard_map/scatter/pallas_call | solution.py:640
  177.3 0.0 copy-done
  177.3 6.0 %combine.1 = (bf16[512,1536]{1,0:T(8,128)(2,1)}, bf16[512,1536]{1,0:T(8,128)(2,1)}) custom-call(f32[512,1536]{1,0:T(8,128)S(1)} %copy-done, f32[512,1536]{1,0:T(8,128)} %get-tuple-element.26.dv, bf16[2,512,1536]{2,1,0:T(8,128)(2,1)} %get-tuple-element.33.ahead, bf16[2,512,1536]{2,1,0:T(8,128)(2,1)} %get-tuple-element.34.behind), custom_call_target="tpu_custom_call" | custom-call | tf_op jit(solution)/shard_map/combine/pallas_call | solution.py:663
  183.3 0.7 copy.16
Async XLA Ops:
  0.6 90.6 %copy-start.7 = (s32[12,3]{0,1:T(4,128)S(1)}, s32[12,3]{0,1:T(4,128)}, u32[]{:S(2)}) copy-start(s32[12,3]{0,1:T(4,128)} %param.17) | copy-start | bytes 436
  0.6 90.7 %copy-start.8 = (s32[64,3]{0,1:T(4,128)S(1)}, s32[64,3]{0,1:T(4,128)}, u32[]{:S(2)}) copy-start(s32[64,3]{0,1:T(4,128)} %param.16) | copy-start | bytes 2308
  0.7 90.8 %copy-start.1 = (bf16[1,512,1536]{2,1,0:T(8,128)(2,1)S(1)}, bf16[1,512,1536]{2,1,0:T(8,128)(2,1)}, u32[]{:S(2)}) copy-start(bf16[1,512,1536]{2,1,0:T(8,128)(2,1)} %param.9) | copy-start | bytes 4718596
  0.7 90.8 %copy-start.2 = (bf16[1,512,1536]{2,1,0:T(8,128)(2,1)S(1)}, bf16[1,512,1536]{2,1,0:T(8,128)(2,1)}, u32[]{:S(2)}) copy-start(bf16[1,512,1536]{2,1,0:T(8,128)(2,1)} %param.10) | copy-start | bytes 4718596
  0.7 90.8 %copy-start.4 = (f32[1,12,512]{2,0,1:T(1,128)S(1)}, f32[1,12,512]{2,0,1:T(1,128)}, u32[]{:S(2)}) copy-start(f32[1,12,512]{2,0,1:T(1,128)} %param.13) | copy-start | bytes 73732
  90.2 29.8 %collective-permute-start = (bf16[2,4,96,768]{3,2,1,0:T(8,128)(2,1)}, bf16[2,4,96,768]{3,2,1,0:T(8,128)(2,1)}, u32[]{:S(2)}, u32[]{:S(2)}) collective-permute-start(bf16[2,4,96,768]{3,2,1,0:T(8,128)(2,1)} %get-tuple-element.30), channel_id=1, source_target_pairs={{0,64},{16,80},{32,96},{48,112},{64,0},{80,16},{96,32},{112,48},{1... | collective-permute-start | bytes 3538952 | tf_op jit(solution)/shard_map/ppermute | solution.py:568
  91.3 28.7 %collective-permute-start.1 = (bf16[2,4,96,768]{3,2,1,0:T(8,128)(2,1)}, bf16[2,4,96,768]{3,2,1,0:T(8,128)(2,1)}, u32[]{:S(2)}, u32[]{:S(2)}) collective-permute-start(bf16[2,4,96,768]{3,2,1,0:T(8,128)(2,1)} %get-tuple-element.32), channel_id=1, source_target_pairs={{0,8},{1,9},{2,10},{3,11},{4,12},{5,13},{6,14},{7,15},{8,0},{9,1},... | collective-permute-start | bytes 3538952 | tf_op jit(solution)/shard_map/ppermute | solution.py:564
  91.5 1.4 copy-start.3
  92.9 27.1 %copy-start.5 = (bf16[2,4,96,768]{3,2,1,0:T(8,128)(2,1)S(1)}, bf16[2,4,96,768]{3,2,1,0:T(8,128)(2,1)}, u32[]{:S(2)}) copy-start(bf16[2,4,96,768]{3,2,1,0:T(8,128)(2,1)} %get-tuple-element.29.keep_a_in) | copy-start | bytes 3538948
  92.9 27.1 %copy-start.6 = (bf16[2,4,96,768]{3,2,1,0:T(8,128)(2,1)S(1)}, bf16[2,4,96,768]{3,2,1,0:T(8,128)(2,1)}, u32[]{:S(2)}) copy-start(bf16[2,4,96,768]{3,2,1,0:T(8,128)(2,1)} %get-tuple-element.31.keep_b_in) | copy-start | bytes 3538948
  120.0 57.3 %copy-start = (f32[512,1536]{1,0:T(8,128)S(1)}, f32[512,1536]{1,0:T(8,128)}, u32[]{:S(2)}) copy-start(f32[512,1536]{1,0:T(8,128)} %get-tuple-element.25.dk) | copy-start | bytes 9437188

commit v3 on v2

--- a/solution.py
+++ b/solution.py
@@ -1,3 +1,4 @@
+import functools
 import functools
 import math
 
@@ -18,12 +19,14 @@
 ROWS = 12
 PAD = 16
 BLK = 8 * ROWS
-CUT = 1152
+CUT = 1024
 PARTS = ((0, CUT), (CUT, HALF))
 SUM_CUT = 768
 SUM_PARTS = ((0, SUM_CUT), (SUM_CUT, HALF))
 SUB = SUM_CUT // 2
 STEPS = (1, 3, 2)
+GROUP = 2
+VMEM_LIMIT = 60 * 2**20
 MESH = pl.DeviceIdType.MESH
 F32 = jnp.float32
 BF16 = jnp.bfloat16
@@ -79,57 +82,74 @@
     pl.semaphore_wait(barrier, 13 + jnp.where((ctx == 7) | (ctx == 8), 1, 0))
 
 
-def halo_copies(pairs, send, recv):
-    dp, ctx = lax.axis_index("dp"), lax.axis_index("ctx")
-    up = jnp.minimum(ctx + 1, 15)
-    down = jnp.maximum(ctx - 1, 0)
-    half = len(pairs) // 2
-    return [
-        remote(src, dst, send.at[i], recv.at[i], (dp, up if i < half else down))
-        for i, (src, dst) in enumerate(pairs)
-    ]
-
-
-def halo_start(copies):
-    ctx = lax.axis_index("ctx")
-    half = len(copies) // 2
-
-    @pl.when(ctx < 15)
-    def _():
-        for copy in copies[:half]:
-            copy.start()
-
-    @pl.when(ctx > 0)
-    def _():
-        for copy in copies[half:]:
-            copy.start()
-
-
-def halo_wait(copies):
-    ctx = lax.axis_index("ctx")
-    half = len(copies) // 2
-
-    @pl.when(ctx < 15)
-    def _():
-        for copy in copies[:half]:
-            copy.wait_send()
-        for copy in copies[half:]:
-            copy.wait_recv()
-
-    @pl.when(ctx > 0)
-    def _():
-        for copy in copies[half:]:
-            copy.wait_send()
-        for copy in copies[:half]:
-            copy.wait_recv()
+HALO_SEMS = [pltpu.SemaphoreType.DMA(shape) for shape in ((2,), (2,), (2, 4), (2, 4), (2, 4))]
+
+
+class Halo:
+    def __init__(self, ups, downs, before, after, send, recv, piece_send, piece_recv, relay_send):
+        self.dp, self.ctx = lax.axis_index("dp"), lax.axis_index("ctx")
+        ctx = self.ctx
+        ways = (
+            (ups, before, jnp.minimum(ctx + 1, 15), jnp.where(ctx == 7, 0, jnp.minimum(ctx + 1, 15)), 8),
+            (downs, after, jnp.maximum(ctx - 1, 0), jnp.where(ctx == 8, 15, jnp.maximum(ctx - 1, 0)), 7),
+        )
+        self.straight, self.pieces, self.relays = [], [], []
+        for i, (src, dst, near, first, last) in enumerate(ways):
+            self.straight.append(
+                remote(src[0], dst.at[0], send.at[i], recv.at[i], (self.dp, near)))
+            spans = [pl.ds(j * TILE, TILE) for j in range(TOK // TILE)]
+            self.pieces.append([
+                remote(src[1].at[span], dst.at[1, span], piece_send.at[i, j], piece_recv.at[i, j],
+                       (self.dp, first)) for j, span in enumerate(spans)])
+            self.relays.append([
+                remote(dst.at[1, span], dst.at[1, span], relay_send.at[i, j], piece_recv.at[i, j],
+                       (self.dp, last)) for j, span in enumerate(spans)])
+        self.sends = (ctx < 15, ctx > 0)
+        self.gets = (ctx > 0, ctx < 15)
+        self.passes = (ctx == 0, ctx == 15)
+
+    def start(self):
+        for i in range(2):
+            @pl.when(self.sends[i])
+            def _():
+                for copy in self.pieces[i]:
+                    copy.start()
+                self.straight[i].start()
+
+    def relay(self, *numbers):
+        for i in range(2):
+            @pl.when(self.passes[i])
+            def _():
+                for j in numbers:
+                    self.pieces[i][j].wait_recv()
+                    self.relays[i][j].start()
+
+    def wait(self):
+        for i in range(2):
+            @pl.when(self.gets[i])
+            def _():
+                self.straight[i].wait_recv()
+                for copy in self.pieces[i]:
+                    copy.wait_recv()
+
+            @pl.when(self.sends[i])
+            def _():
+                self.straight[i].wait_send()
+                for copy in self.pieces[i]:
+                    copy.wait_send()
+
+            @pl.when(self.passes[i])
+            def _():
+                for onward in self.relays[i]:
+                    onward.wait_send()
 
 
 def gather_kernel(
     strip, keys, vals, so_hbm, og_hbm,
     before, after, d_attn_out, keep_a_out, send_a_out, keep_b_out, send_b_out,
-    strips, full, so, og, so_sib, og_sib, turn, d_attn, keep_a, send_a, keep_b, send_b,
+    padded, strips, full, so, og, so_sib, og_sib, turn, d_attn, keep_a, send_a, keep_b, send_b,
     strip_send, strip_recv, near_send, far_send, pass_send, ag_recv, late_recv, sib_send, sib_recv,
-    ex_send, ex_recv, halo_send, halo_recv, load_sem, store_sem,
+    ex_send, ex_recv, load_sem, store_sem, *halo_sems,
 ):
     z, x, y, c = place()
     sib = device(z, x, y, 1 - c)
@@ -139,8 +159,10 @@
              pltpu.make_async_copy(og_hbm, og, load_sem.at[1])]
     for copy in loads:
         copy.start()
-    strips[slot, 0:ROWS] = strip[...]
-    strips[slot, ROWS:PAD] = jnp.zeros((PAD - ROWS, D), BF16)
+    for h in range(2):
+        padded[h, 0:ROWS] = strip[:, h * HALF:(h + 1) * HALF]
+        padded[h, ROWS:PAD] = jnp.zeros((PAD - ROWS, HALF), BF16)
+    strips[slot] = padded[c]
     greet(z, x, y, c)
 
     pending = []
@@ -148,8 +170,9 @@
     for dy in range(4):
         for dc in range(2):
             if dy or dc:
-                copy = remote(strips.at[slot], strips.at[slot], strip_send.at[number],
-                              strip_recv.at[slot], device(z, x, (y + dy) % 4, (c + dc) % 2))
+                tc = (c + dc) % 2
+                copy = remote(padded.at[tc], strips.at[slot], strip_send.at[number],
+                              strip_recv.at[slot], device(z, x, (y + dy) % 4, tc))
                 copy.start()
                 pending.append(copy)
                 number += 1
@@ -169,11 +192,10 @@
     row = lax.broadcasted_iota(jnp.int32, (BLK, 8 * PAD), 0)
     col = lax.broadcasted_iota(jnp.int32, (BLK, 8 * PAD), 1)
     pick = jnp.where(col == (row // ROWS) * PAD + row % ROWS, 1.0, 0.0).astype(BF16)
-    for h in range(2):
-        for o in range(0, HALF, 768):
-            full[h, me, :, o:o + 768] = jnp.dot(
-                pick, strips[:, :, h * HALF + o:h * HALF + o + 768].reshape(8 * PAD, 768),
-                preferred_element_type=F32).astype(BF16)
+    for o in range(0, HALF, 768):
+        full[c, me, :, o:o + 768] = jnp.dot(
+            pick, strips[:, :, o:o + 768].reshape(8 * PAD, 768),
+            preferred_element_type=F32).astype(BF16)
 
     def piece(half, block, part):
         low, high = PARTS[part]
@@ -232,11 +254,10 @@
 
     for part in range(2):
         onward(part, me, 0)
-
-    halos = halo_copies(
-        [(keys, before.at[0]), (vals, before.at[1]), (keys, after.at[0]), (vals, after.at[1])],
-        halo_send, halo_recv)
-    halo_start(halos)
+        to_sibling(part, me)
+
+    halo = Halo((keys, vals), (keys, vals), before, after, *halo_sems)
+    halo.start()
     for copy in exchange:
         copy.wait_recv()
     for copy in loads:
@@ -271,43 +292,48 @@
                 first[1, group, :, :SUB] = total[:, :SUB]
                 other[1, group, :, SUB:] = total[:, SUB:]
 
+    wgrad_group(z, 0)
     for j, step in enumerate(STEPS):
         for part in range(2):
             block = block_at(part, True, step)
             arrived(part, block)
             onward(part, block, j + 1)
             to_sibling(part, block)
-    for j in range(4):
-        wgrad_group((z + j) % 4, j)
+        wgrad_group((z + j + 1) % 4, j + 1)
+    halo.relay(0)
     stores = []
     for j, (src, dst) in enumerate(((keep_a, keep_a_out), (send_a, send_a_out),
                                     (keep_b, keep_b_out), (send_b, send_b_out))):
         stores.append(pltpu.make_async_copy(src, dst, store_sem.at[j]))
         stores[-1].start()
 
-    for step in STEPS:
-        for j, inner in enumerate((0,) + STEPS):
+    def far_block(part, step, inner):
+        if part == 0:
+            return block_of((z + step) % 4, (x + inner) % 4)
+        return block_of((z + inner) % 4, (x + step) % 4)
+
+    for j, inner in enumerate((0,) + STEPS):
+        for step in (1, 3):
             for part in range(2):
-                if part == 0:
-                    block = block_of((z + step) % 4, (x + inner) % 4)
-                else:
-                    block = block_of((z + inner) % 4, (x + step) % 4)
-                if step == 2:
-                    arrived_late(part, block)
-                else:
-                    arrived(part, block)
-                    pass_on(part, block, j, step)
+                block = far_block(part, step, inner)
+                arrived(part, block)
+                pass_on(part, block, j, step)
                 to_sibling(part, block)
+        if j:
+            halo.relay(j)
+    for inner in (0,) + STEPS:
+        for part in range(2):
+            block = far_block(part, 2, inner)
+            arrived_late(part, block)
+            to_sibling(part, block)
 
     for step in (0,) + STEPS:
         group = (z + step) % 4
         for inner in range(4):
             block = group * 4 + inner
             for part in range(2):
-                @pl.when(block != me)
-                def _():
-                    remote(piece(1 - c, block, part), piece(1 - c, block, part),
-                           sib_send.at[part, block], sib_recv.at[part, block], sib).wait_recv()
+                remote(piece(1 - c, block, part), piece(1 - c, block, part),
+                       sib_send.at[part, block], sib_recv.at[part, block], sib).wait_recv()
         feats = pl.ds(pl.multiple_of(group * 4 * BLK, 4 * BLK), 4 * BLK)
 
         def project(i, carry):
@@ -324,7 +350,7 @@
         stores.append(pltpu.make_async_copy(d_attn.at[:, feats], d_attn_out.at[:, feats],
                                             store_sem.at[4 + step]))
         stores[-1].start()
-    halo_wait(halos)
+    halo.wait()
     for copy in stores:
         copy.wait()
     for copy in exchange:
@@ -339,7 +365,7 @@
     keep_a, got_a, keep_b, got_b, pass_a, pass_b, more_a, more_b,
     sum_a, sum_b, got_a2, got_b2, packed, last,
     first_send, first_recv, second_send, second_recv, last_send, last_recv,
-    halo_send, halo_recv, load_sem,
+    load_sem, *halo_sems,
 ):
     z, x, y, c = place()
     slot = y * 2 + c
@@ -350,7 +376,8 @@
         loads.append(pltpu.make_async_copy(src, dst, load_sem.at[j]))
         loads[-1].start()
     greet(z, x, y, c)
-    halos = halo_copies([(to_next, from_prev), (to_prev, from_next)], halo_send, halo_recv)
+    halo = Halo((to_next.at[0], to_next.at[1]), (to_prev.at[0], to_prev.at[1]),
+                from_prev, from_next, *halo_sems)
     for copy in loads:
         copy.wait()
     first = []
@@ -364,7 +391,7 @@
                           first_recv.at[part, i], target)
             copy.start()
             first.append(copy)
-    halo_start(halos)
+    halo.start()
     for copy in first:
         copy.wait_recv()
     for keep, got, more, total_ref in (
@@ -383,6 +410,7 @@
             copy = remote(src, dst, second_send.at[part, i], second_recv.at[part, i], target)
             copy.start()
             second.append(copy)
+    halo.relay(0, 1)
     for copy in second:
         copy.wait_recv()
     row = lax.broadcasted_iota(jnp.int32, (8 * PAD, BLK), 0)
@@ -409,6 +437,7 @@
                 copy.start()
                 third.append(copy)
                 number += 1
+    halo.relay(2, 3)
     last[slot] = packed[slot]
     for dy in range(4):
         for dc in range(2):
@@ -421,22 +450,20 @@
         for i in range(1, 4):
             total += last[2 * i + h].astype(F32)
         out[:, h * HALF:(h + 1) * HALF] = total[:ROWS] * (1.0 / 256.0)
-    halo_wait(halos)
+    halo.wait()
     for copy in first + second + third:
         copy.wait_send()
 
 
 def attention_kernel(
-    coords, extents,
-    q_ref, k_ref, v_ref, kp_ref, vp_ref, kn_ref, vn_ref, a_ref, o_ref, lse_ref,
-    dq_ref, dk_ref, dv_ref, prev_ref, next_ref,
-    table, q_s, a_s, k_s, v_s, kt_s, row_s, dqt_s,
+    first, coords, extents,
+    q_all, k_all, v_all, kp_all, vp_all, kn_all, vn_all, a_all, o_all, lse_all, *refs,
 ):
-    head = pl.program_id(0)
+    outputs, (table, row_s, dqt_s) = refs[-8:-3], refs[-3:]
+    begin = first + pl.program_id(0) * GROUP
     frame = lax.axis_index("ctx")
-    scale = HEAD ** (-0.5)
-
-    @pl.when(head == 0)
+
+    @pl.when(begin == first)
     def _():
         for k in range(3):
             base = jnp.clip(frame + k - 1, 0, 15) * 4
@@ -445,105 +472,139 @@
                 table[0, k, r * 2 + col] = t
                 table[1, k, col * 2 + r] = t
 
+    def one_head(j, carry):
+        cols = pl.ds(pl.multiple_of(j * HEAD, HEAD), HEAD)
+        flat = [ref.at[:, cols] for ref in (
+            q_all, k_all, v_all, kp_all, vp_all, kn_all, vn_all, a_all, o_all) + outputs[:3]]
+        sides = [ref.at[:, :, cols] for ref in outputs[3:]]
+        head_kernel(begin + j, frame, extents, *flat[:9], lse_all.at[j], *flat[9:], *sides,
+                    table, row_s, dqt_s)
+        return carry
+
+    lax.fori_loop(0, GROUP, one_head, 0)
+
+
+def head_kernel(
+    head, frame, extents,
+    q_ref, k_ref, v_ref, kp_ref, vp_ref, kn_ref, vn_ref, a_ref, o_ref, lse_ref,
+    dq_ref, dk_ref, dv_ref, prev_ref, next_ref, table, row_s, dqt_s,
+):
+    scale = HEAD ** (-0.5)
     near_f, near_r, near_c = extents[head, 0], extents[head, 1], extents[head, 2]
     order = jnp.where(near_c == 0, 1, 0)
-
-    def rows(k, s):
+    keys, vals = (kp_ref, k_ref, kn_ref), (vp_ref, v_ref, vn_ref)
+    outs = ((prev_ref.at[0], prev_ref.at[1]), (dk_ref, dv_ref), (next_ref.at[0], next_ref.at[1]))
+
+    def spot(k, s):
         return pl.ds(pl.multiple_of(table[order, k, s] * TILE, TILE), TILE)
 
-    for s in range(4):
-        own = rows(1, s)
-        here = slice(s * TILE, (s + 1) * TILE)
-        q_s[here, :] = q_ref[own, :]
-        a_tile = a_ref[own, :]
-        a_s[here, :] = a_tile
-        prod = a_tile.astype(F32) * o_ref[own, :].astype(F32)
-        row_s[0:1, here] = lse_ref[:, own] * LOG2E
-        row_s[1:2, here] = jnp.sum(prod.T, axis=0, keepdims=True)
-    sources = ((kp_ref, vp_ref), (k_ref, v_ref), (kn_ref, vn_ref))
-
-    def load(k):
-        for s in range(4):
-            here = slice(s * TILE, (s + 1) * TILE)
-            tile = sources[k][0][rows(k, s), :]
-            k_s[k, here, :] = tile
-            kt_s[k, :, here] = tile.T
-            v_s[k, here, :] = sources[k][1][rows(k, s), :]
-
-    def put(k, s, dk, dv):
-        if k == 1:
-            dk_ref[rows(k, s), :] = dk
-            dv_ref[rows(k, s), :] = dv
-        elif k == 0:
-            prev_ref[0, rows(k, s), :] = dk.astype(BF16)
-            prev_ref[1, rows(k, s), :] = dv.astype(BF16)
-        else:
-            next_ref[0, rows(k, s), :] = dk.astype(BF16)
-            next_ref[1, rows(k, s), :] = dv.astype(BF16)
-
-    def unit(k, begin, size):
-        span = slice(begin, begin + size)
-        q, a = q_s[span, :], a_s[span, :]
-        lse, delta = row_s[0:1, span], row_s[1:2, span]
+    def rows_of(ref, k, begin, size, whole):
+        if whole:
+            return ref[begin:begin + size, :]
+        tiles = [ref[spot(k, s), :] for s in range(begin // TILE, (begin + size) // TILE)]
+        return tiles[0] if len(tiles) == 1 else jnp.concatenate(tiles, axis=0)
+
+    def line_of(i, begin, size, whole):
+        if whole:
+            return row_s[i:i + 1, begin:begin + size]
+        tiles = [row_s[i:i + 1, spot(1, s)] for s in range(begin // TILE, (begin + size) // TILE)]
+        return tiles[0] if len(tiles) == 1 else jnp.concatenate(tiles, axis=1)
+
+    def frame_of(k, size):
+        whole = size == TOK
         step = min(size, 256)
-        total = None
-        for at in range(begin, begin + size, step):
-            part = slice(at, at + step)
-            scores = lax.dot_general(k_s[k, part, :], q, NT, preferred_element_type=F32)
+        queries = [
+            (rows_of(q_ref, 1, at, size, whole), rows_of(a_ref, 1, at, size, whole),
+             line_of(0, at, size, whole), line_of(1, at, size, whole))
+            for at in range(0, TOK, size)]
+        units = [(g, at) for g in range(TOK // size) for at in range(g * size, (g + 1) * size, step)]
+        ready = []
+        for g, at in units:
+            q, a, lse, delta = queries[g]
+            key = rows_of(keys[k], k, at, step, whole)
+            scores = lax.dot_general(key, q, NT, preferred_element_type=F32)
+            d_probs = lax.dot_general(rows_of(vals[k], k, at, step, whole), a, NT,
+                                      preferred_element_type=F32)
+            ready.append((key, scores, d_probs))
+        halves = []
+        for (g, at), (key, scores, d_probs) in zip(units, ready):
+            q, a, lse, delta = queries[g]
             probs = jnp.exp2(scores * (scale * LOG2E) - lse)
-            d_probs = lax.dot_general(v_s[k, part, :], a, NT, preferred_element_type=F32)
-            d_scores = (probs * (d_probs - delta)).astype(BF16)
-            dv = jnp.dot(probs.astype(BF16), a, preferred_element_type=F32)
+            halves.append((probs.astype(BF16), (probs * (d_probs - delta)).astype(BF16)))
+        sums = [None] * (TOK // size)
+        for (g, at), (key, _, _), (probs, d_scores) in zip(units, ready, halves):
+            q, a, lse, delta = queries[g]
+            dv = jnp.dot(probs, a, preferred_element_type=F32)
             dk = jnp.dot(d_scores, q, preferred_element_type=F32) * scale
-            dqt = jnp.dot(kt_s[k, :, part], d_scores, preferred_element_type=F32)
-            total = dqt if total is None else total + dqt
-            for i in range(step // TILE):
-                cut = slice(i * TILE, (i + 1) * TILE)
-                put(k, at // TILE + i, dk[cut], dv[cut])
-        if k == 1:
-            dqt_s[:, span] = total
-        else:
-            dqt_s[:, span] += total
-
-    def frame_of(k):
-        load(k)
-
-        @pl.when(near_r * near_c == 1)
+            dqt = jnp.dot(key.T, d_scores, preferred_element_type=F32)
+            sums[g] = dqt if sums[g] is None else sums[g] + dqt
+            for ref, value in zip(outs[k], (dk, dv)):
+                if whole:
+                    ref[at:at + step, :] = value.astype(ref.dtype)
+                else:
+                    for i in range(step // TILE):
+                        ref[spot(k, at // TILE + i), :] = value[i * TILE:(i + 1) * TILE].astype(
+                            ref.dtype)
+        for g, total in enumerate(sums):
+            span = slice(g * size, (g + 1) * size)
+            if k == 1:
+                dqt_s[:, span] = total
+            else:
+                dqt_s[:, span] += total
+
+    wide = near_r * near_c == 1
+    modes = ((TOK, wide), (256, near_r + near_c == 1), (TILE, near_r + near_c == 0))
+    ones = jnp.ones((8, HEAD), BF16)
+    prod = a_ref[...].astype(F32) * o_ref[...].astype(F32)
+    high = prod.astype(BF16)
+    low = (prod - high.astype(F32)).astype(BF16)
+    delta = lax.dot_general(ones, high, NT, preferred_element_type=F32)
+    delta += lax.dot_general(ones, low, NT, preferred_element_type=F32)
+    row_s[0:1, :] = lse_ref[...] * LOG2E
+    row_s[1:2, :] = delta[0:1]
+    for size, here in modes:
+        @pl.when(here)
         def _():
-            unit(k, 0, 512)
-
-        @pl.when(near_r + near_c == 1)
-        def _():
-            for g in range(2):
-                unit(k, g * 256, 256)
-
-        @pl.when(near_r + near_c == 0)
-        def _():
-            for g in range(4):
-                unit(k, g * 128, 128)
-
-    frame_of(1)
+            frame_of(1, size)
+
     for k, there, ref in ((0, frame > 0, prev_ref), (2, frame < 15, next_ref)):
         use = (near_f == 1) & there
-
-        @pl.when(use)
-        def _():
-            frame_of(k)
+        for size, here in modes:
+            @pl.when(use & here)
+            def _():
+                frame_of(k, size)
 
         @pl.when(jnp.logical_not(use))
         def _():
             ref[...] = jnp.zeros_like(ref)
 
-    for s in range(4):
-        dq_ref[rows(1, s), :] = (dqt_s[:, s * TILE:(s + 1) * TILE].T * scale).astype(BF16)
-
-
-def combine_kernel(dk, dv, ahead, behind, key_out, value_out):
+    @pl.when(wide)
+    def _():
+        dq_ref[...] = (dqt_s[...].T * scale).astype(BF16)
+
+    @pl.when(jnp.logical_not(wide))
+    def _():
+        for s in range(4):
+            dq_ref[spot(1, s), :] = (dqt_s[:, s * TILE:(s + 1) * TILE].T * scale).astype(BF16)
+
+
+def combine_kernel(dk, dv, ahead0, behind0, ahead1, behind1, key_out, value_out):
+    step = pl.program_id(0)
     frame = lax.axis_index("ctx")
-    for i, (own, out) in enumerate(((dk, key_out), (dv, value_out))):
-        total = own[...] + jnp.where(frame < 15, ahead[i].astype(F32), 0.0)
-        total += jnp.where(frame > 0, behind[i].astype(F32), 0.0)
-        out[...] = total.astype(BF16)
+
+    def put(ahead, behind):
+        for i, (own, out) in enumerate(((dk, key_out), (dv, value_out))):
+            total = own[...] + jnp.where(frame < 15, ahead[i].astype(F32), 0.0)
+            total += jnp.where(frame > 0, behind[i].astype(F32), 0.0)
+            out[...] = total.astype(BF16)
+
+    @pl.when(step < 2)
+    def _():
+        put(ahead0, behind0)
+
+    @pl.when(step >= 2)
+    def _():
+        put(ahead1, behind1)
 
 
 def any_spec():
@@ -572,7 +633,6 @@
     queries, key_rows, values, saved_out, log_sum, out_grad, out_weight, tile_coords, extents
 ):
     q, k, v, so, og = (a[0] for a in (queries, key_rows, values, saved_out, out_grad))
-    col = pl.BlockSpec((TOK, HEAD), lambda h, *_: (0, h))
     pair = jax.ShapeDtypeStruct((2, TOK, HD), BF16)
     dma = pltpu.SemaphoreType.DMA
     moving = jax.ShapeDtypeStruct((2, 4, BLK, SUM_CUT), BF16)
@@ -582,7 +642,8 @@
         in_specs=[vmem_spec()] + [any_spec()] * 4,
         out_specs=(any_spec(),) * 7,
         scratch_shapes=[
-            pltpu.VMEM((8, PAD, D), BF16),
+            pltpu.VMEM((2, PAD, HALF), BF16),
+            pltpu.VMEM((8, PAD, HALF), BF16),
             pltpu.VMEM((2, 16, BLK, HALF), BF16),
             pltpu.VMEM((TOK, HD), BF16),
             pltpu.VMEM((TOK, D), BF16),
@@ -592,11 +653,10 @@
             pltpu.VMEM((TOK, HD), BF16),
         ] + [pltpu.VMEM((2, 4, BLK, SUM_CUT), BF16)] * 4 + [
             dma((7,)), dma((8,)), dma((2, 3)), dma((2, 4, 2)), dma((2, 4, 2)), dma((2, 16)),
-            dma((2, 16)), dma((2, 16)), dma((2, 16)), dma((2,)), dma((2,)), dma((4,)), dma((4,)),
-            dma((2,)), dma((8,)),
-        ],
+            dma((2, 16)), dma((2, 16)), dma((2, 16)), dma((2,)), dma((2,)), dma((2,)), dma((8,)),
+        ] + HALO_SEMS,
         compiler_params=pltpu.CompilerParams(
-            collective_id=0, has_side_effects=True, vmem_limit_bytes=56 * 2**20),
+            collective_id=0, has_side_effects=True, vmem_limit_bytes=VMEM_LIMIT),
         cost_estimate=pl.CostEstimate(
             flops=10**10, bytes_accessed=20 * 10**6, transcendentals=0),
         name="gather",
@@ -605,41 +665,45 @@
 
     own32 = jax.ShapeDtypeStruct((TOK, HD), F32)
     own16 = jax.ShapeDtypeStruct((TOK, HD), BF16)
-    row = pl.BlockSpec((None, 1, TOK), lambda h, *_: (h, 0, 0))
-
-    def side(i):
-        return pl.BlockSpec((None, TOK, HEAD), lambda h, *_, i=i: (i, 0, h))
-
-    sides = pl.BlockSpec((2, TOK, HEAD), lambda h, *_: (0, 0, h))
-    dq, dk, dv, to_prev, to_next = pl.pallas_call(
-        attention_kernel,
-        out_shape=(own16, own32, own32, pair, pair),
-        grid_spec=pltpu.PrefetchScalarGridSpec(
-            num_scalar_prefetch=2,
-            grid=(H,),
-            in_specs=[col] * 3 + [side(0), side(1)] * 2 + [col] * 2 + [row],
-            out_specs=(col,) * 3 + (sides,) * 2,
-            scratch_shapes=[
-                pltpu.SMEM((2, 3, 4), jnp.int32),
-                pltpu.VMEM((TOK, HEAD), BF16),
-                pltpu.VMEM((TOK, HEAD), BF16),
-                pltpu.VMEM((3, TOK, HEAD), BF16),
-                pltpu.VMEM((3, TOK, HEAD), BF16),
-                pltpu.VMEM((3, HEAD, TOK), BF16),
-                pltpu.VMEM((8, TOK), F32),
-                pltpu.VMEM((HEAD, TOK), F32),
-            ],
-        ),
-        compiler_params=pltpu.CompilerParams(vmem_limit_bytes=48 * 2**20),
-        cost_estimate=pl.CostEstimate(
-            flops=12 * 10**9, bytes_accessed=30 * 10**6, transcendentals=10**7),
-        name="attention",
-    )(tile_coords, extents, q, k, v, before, before, after, after, d_attn, so,
-      log_sum[0][:, None, :])
+    half_pair = jax.ShapeDtypeStruct((2, TOK, HD // 2), BF16)
+    grads, towards = (), []
+    for first in (0, H // 2):
+        skip, wide = first // GROUP, GROUP * HEAD
+        col = pl.BlockSpec((TOK, wide), lambda h, *_, skip=skip: (0, skip + h))
+        row = pl.BlockSpec((GROUP, 1, TOK), lambda h, *_, skip=skip: (skip + h, 0, 0))
+        sides = pl.BlockSpec((2, TOK, wide), lambda h, *_: (0, 0, h))
+        k_side = pl.BlockSpec((None, TOK, wide), lambda h, *_, skip=skip: (0, 0, skip + h))
+        v_side = pl.BlockSpec((None, TOK, wide), lambda h, *_, skip=skip: (1, 0, skip + h))
+        *grads, to_prev, to_next = pl.pallas_call(
+            functools.partial(attention_kernel, first),
+            out_shape=(own16, own32, own32, half_pair, half_pair),
+            grid_spec=pltpu.PrefetchScalarGridSpec(
+                num_scalar_prefetch=2,
+                grid=(H // 2 // GROUP,),
+                in_specs=[col] * 3 + [k_side, v_side] * 2 + [col] * 2 + [row]
+                + [any_spec()] * len(grads),
+                out_specs=(col,) * 3 + (sides,) * 2,
+                scratch_shapes=[
+                    pltpu.SMEM((2, 3, 4), jnp.int32),
+                    pltpu.VMEM((8, TOK), F32),
+                    pltpu.VMEM((HEAD, TOK), F32),
+                ],
+            ),
+            input_output_aliases={12 + i: i for i in range(len(grads))},
+            compiler_params=pltpu.CompilerParams(vmem_limit_bytes=VMEM_LIMIT),
+            cost_estimate=pl.CostEstimate(
+                flops=6 * 10**9, bytes_accessed=15 * 10**6, transcendentals=5 * 10**6),
+            name="attention",
+        )(tile_coords, extents, q, k, v, before, before, after, after, d_attn, so,
+          log_sum[0][:, None, :], *grads)
+        towards.append((to_prev, to_next))
+    dq, dk, dv = grads
+    ahead = lax.ppermute(towards[0][0], "ctx", [(i + 1, i) for i in range(15)])
+    behind = lax.ppermute(towards[0][1], "ctx", [(i, i + 1) for i in range(15)])
 
     weight_grad, from_next, from_prev = pl.pallas_call(
         scatter_kernel,
-        out_shape=(jax.ShapeDtypeStruct((ROWS, D), F32), pair, pair),
+        out_shape=(jax.ShapeDtypeStruct((ROWS, D), F32), half_pair, half_pair),
         in_specs=[any_spec()] * 6,
         out_specs=(vmem_spec(), any_spec(), any_spec()),
         scratch_shapes=[pltpu.VMEM((2, 4, BLK, SUM_CUT), BF16)] * 4
@@ -648,27 +712,28 @@
             pltpu.VMEM((8, PAD, HALF), BF16),
             pltpu.VMEM((8, PAD, HALF), BF16),
             dma((2, 2)), dma((2, 2)), dma((2, 3)), dma((2, 3)), dma((7,)), dma((8,)),
-            dma((2,)), dma((2,)), dma((4,)),
-        ],
+            dma((4,)),
+        ] + HALO_SEMS,
         compiler_params=pltpu.CompilerParams(
-            collective_id=1, has_side_effects=True, vmem_limit_bytes=48 * 2**20),
+            collective_id=1, has_side_effects=True, vmem_limit_bytes=VMEM_LIMIT),
         cost_estimate=pl.CostEstimate(
             flops=10**10, bytes_accessed=20 * 10**6, transcendentals=0),
         name="scatter",
-    )(to_prev, to_next, keep_a, got_a, keep_b, got_b)
+    )(*towards[1], keep_a, got_a, keep_b, got_b)
 
     wide = HD // 4
     whole = pl.BlockSpec((TOK, wide), lambda i: (0, i))
-    halo = pl.BlockSpec((2, TOK, wide), lambda i: (0, 0, i))
+    lower = pl.BlockSpec((2, TOK, wide), lambda i: (0, 0, jnp.minimum(i, 1)))
+    upper = pl.BlockSpec((2, TOK, wide), lambda i: (0, 0, jnp.maximum(i - 2, 0)))
     key_grad, value_grad = pl.pallas_call(
         combine_kernel,
         out_shape=(own16, own16),
         grid=(4,),
-        in_specs=[whole, whole, halo, halo],
+        in_specs=[whole, whole, lower, lower, upper, upper],
         out_specs=(whole, whole),
-        compiler_params=pltpu.CompilerParams(vmem_limit_bytes=48 * 2**20),
+        compiler_params=pltpu.CompilerParams(vmem_limit_bytes=VMEM_LIMIT),
         name="combine",
-    )(dk, dv, from_next, from_prev)
+    )(dk, dv, ahead, behind, from_next, from_prev)
     return dq[None], key_grad[None], value_grad[None], weight_grad
 
 

time: 186 us -> 153 us (0.82)
  Pallas kernels: 180 us -> 141 us
  starting transfers between devices: 1.08 us -> 6.62 us
    pallas_call x1, Pallas kernels: 89.5 us -> 66.3 us  [shards(): pl.pallas_call(gather_kernel, out_shape=(pair, pair, jax.ShapeDtypeStruct...]
    pallas_call x1, Pallas kernels: 57.3 us -> 39.8 us  [shards(): pl.pallas_call(scatter_kernel, out_shape=(jax.ShapeDtypeStruct((ROWS, D),...]
    ppermute x0 -> x2, starting transfers between devices: none -> 4.33 us  [the longest x1 2.39 us: shards(): ahead = lax.ppermute(towards[0][0], 'ctx', [(i + 1, i) for i in range(15)])]
    unnamed x21 -> x13, local copies, waits for them, and re-layouts: 2.3 us -> 3.72 us
    pallas_call x1 -> x2, Pallas kernels: 27 us -> 28.1 us  [shards(): pl.pallas_call(functools.partial(attention_kernel, first), out_shape=(own...]
  transfers between devices with their start and end apart: 2 -> 4, of which waited for: 0 -> 0; matrix products, arithmetic and copies ran while one was open for 0% -> 1% of each run, Pallas kernels for 15% -> 45%
where the time goes in v3:
time: 153 us; the launch traced here: 152 us
  Pallas kernels  141 us (92%)
  starting transfers between devices  6.62 us (4%)
  local copies, waits for them, and re-layouts  3.72 us (2%)
    pallas_call x1, Pallas kernels, shards(): pl.pallas_call(gather_kernel, out_shape=(pair, pair, jax.ShapeDtypeStruct...  66.3 us
    pallas_call x1, Pallas kernels, shards(): pl.pallas_call(scatter_kernel, out_shape=(jax.ShapeDtypeStruct((ROWS, D),...  39.8 us
    pallas_call x2, Pallas kernels, shards(): pl.pallas_call(functools.partial(attention_kernel, first), out_shape=(own...  28.1 us
    pallas_call x1, Pallas kernels, shards(): pl.pallas_call(combine_kernel, out_shape=(own16, own16), grid=(4,), in_sp...  7.2 us
    unnamed x13, local copies, waits for them, and re-layouts  3.72 us
  transfers between devices with their start and end apart: 4, of which 0 were waited for; matrix products, arithmetic and copies ran while one was open for 1% of the time, Pallas kernels for 45%

profile of v3, /device:TPU:4, one launch (start us, length us, event | category | flops | bytes accessed | tf_op | source)
XLA Modules:
  0.0 152.5 jit_solution(4233796979641660747)
XLA Ops:
  0.6 0.0 copy-start.3
  0.6 0.0 copy-start.4
  0.7 66.3 %gather.1 = (bf16[2,512,1536]{2,1,0:T(8,128)(2,1)}, bf16[2,512,1536]{2,1,0:T(8,128)(2,1)}, bf16[512,1536]{1,0:T(8,128)(2,1)}, bf16[2,4,96,768]{3,2,1,0:T(8,128)(...) custom-call(bf16[12,3072]{1,0:T(8,128)(2,1)} %strip.1, ...), custom_call_target="tpu_custom_call" | custom-call | flops 10000000000 | bytes 20000000 | tf_op jit(solution)/shard_map/gather/pallas_call | solution.py:639
  66.9 1.3 collective-permute-start.2
  68.2 1.0 collective-permute-start.3
  69.2 0.0 copy-done.3
  69.2 0.7 copy.19.extents
  69.9 0.0 copy-done.4
  69.9 0.7 copy.18.coords
  70.6 13.3 %attention.2 = (bf16[512,1536]{1,0:T(8,128)(2,1)}, f32[512,1536]{1,0:T(8,128)}, f32[512,1536]{1,0:T(8,128)}, bf16[2,512,768]{2,1,0:T(8,128)(2,1)}, bf16[2,512,768]{2,1,0:T(8,128)(2,1)}) custom-call(s32[64,3]{1,0:T(8,128)} %copy.18.coords, s32[12,3]{1,0:T(8,128)} %copy.19.extents, bf16[512,1536]{1,0:T(8,128)(2,1)} %bitcast.9, bf16[512,1536]{1,0:T(8,128)(2,1)} %bitcast.12, ...), custom_call_target="tpu_custom_call" | custom-call | flops 6000000000 | bytes 15000000 | tf_op jit(solution)/shard_map/attention/pallas_call | solution.py:677
  83.9 2.4 %collective-permute-start = (bf16[2,512,768]{2,1,0:T(8,128)(2,1)}, bf16[2,512,768]{2,1,0:T(8,128)(2,1)S(1)}, u32[]{:S(2)}, u32[]{:S(2)}) collective-permute-start(bf16[2,512,768]{2,1,0:T(8,128)(2,1)} %get-tuple-element.35), channel_id=1, source_target_pairs={{1,0},{2,1},{3,2},{4,3},{5,4},{6,5},{7,6},{8,7},{9,8},{10,9},{11,1... | collective-permute-start | bytes 4718600 | tf_op jit(solution)/shard_map/ppermute | solution.py:701
  86.3 1.9 %collective-permute-start.1 = (bf16[2,512,768]{2,1,0:T(8,128)(2,1)}, bf16[2,512,768]{2,1,0:T(8,128)(2,1)S(1)}, u32[]{:S(2)}, u32[]{:S(2)}) collective-permute-start(bf16[2,512,768]{2,1,0:T(8,128)(2,1)} %get-tuple-element.36), channel_id=1, source_target_pairs={{0,1},{1,2},{2,3},{3,4},{4,5},{5,6},{6,7},{7,8},{8,9},{9,10},{10,1... | collective-permute-start | bytes 4718600 | tf_op jit(solution)/shard_map/ppermute | solution.py:702
  88.2 14.8 %attention.3 = (bf16[512,1536]{1,0:T(8,128)(2,1)}, f32[512,1536]{1,0:T(8,128)}, f32[512,1536]{1,0:T(8,128)}, bf16[2,512,768]{2,1,0:T(8,128)(2,1)}, bf16[2,512,768]{2,1,0:T(8,128)(2,1)}) custom-call(s32[64,3]{1,0:T(8,128)} %copy.18.coords, s32[12,3]{1,0:T(8,128)} %copy.19.extents, ...), custom_call_target="tpu_custom_call", output_to_operand_aliasing={{0}: (12, {}), {1}: (13, {}), {2}: (14, {})} | custom-call | flops 6000000000 | bytes 15000000 | tf_op jit(solution)/shard_map/attention/pallas_call | solution.py:677
  103.0 0.0 collective-permute-done.2.got_a_in
  103.0 0.0 collective-permute-done.3.got_b_in
  103.1 39.8 %scatter.1 = (f32[12,3072]{1,0:T(8,128)}, bf16[2,512,768]{2,1,0:T(8,128)(2,1)}, bf16[2,512,768]{2,1,0:T(8,128)(2,1)}) custom-call(bf16[2,512,768]{2,1,0:T(8,128)(2,1)} %get-tuple-element.37.to_prev, bf16[2,512,768]{2,1,0:T(8,128)(2,1)} %get-tuple-element.38.to_next, bf16[2,4,96,768]{3,2,1,0:T(8,128)(2,1)} %get-tuple-element.39.keep_a_in, ...), custom_call_target="tpu_custom_call" | custom-call | flops 10000000000 | bytes 20000000 | tf_op jit(solution)/shard_map/scatter/pallas_call | solution.py:704
  142.9 0.0 collective-permute-done.ahead0
  142.9 0.0 copy-start
  142.9 0.0 collective-permute-done.1.behind0
  142.9 0.0 copy-start.1
  142.9 1.1 copy-done
  144.1 0.5 copy-done.1
  144.6 0.0 copy-start.2
  144.6 7.2 %combine.1 = (bf16[512,1536]{1,0:T(8,128)(2,1)}, bf16[512,1536]{1,0:T(8,128)(2,1)}) custom-call(f32[512,1536]{1,0:T(8,128)} %get-tuple-element.33.dk, f32[512,1536]{1,0:T(8,128)} %get-tuple-element.34.dv, bf16[2,512,768]{2,1,0:T(8,128)(2,1)} %copy-done, bf16[2,512,768]{2,1,0:T(8,128)(2,1)} %copy-done.1, bf16[2,512,768]{2,1,0:T(8,128)(2,1)} %get-tuple-element.43.ahead1, ...), custom_call_target="tpu_custom_call" | custom-call | tf_op jit(solution)/shard_map/combine/pallas_call | solution.py:728
  151.8 0.0 copy-done.2
  151.8 0.7 copy.24
Async XLA Ops:
  0.6 68.6 %copy-start.3 = (s32[12,3]{0,1:T(4,128)S(1)}, s32[12,3]{0,1:T(4,128)}, u32[]{:S(2)}) copy-start(s32[12,3]{0,1:T(4,128)} %param.17) | copy-start | bytes 436
  0.6 69.3 %copy-start.4 = (s32[64,3]{0,1:T(4,128)S(1)}, s32[64,3]{0,1:T(4,128)}, u32[]{:S(2)}) copy-start(s32[64,3]{0,1:T(4,128)} %param.16) | copy-start | bytes 2308
  66.9 36.1 %collective-permute-start.2 = (bf16[2,4,96,768]{3,2,1,0:T(8,128)(2,1)}, bf16[2,4,96,768]{3,2,1,0:T(8,128)(2,1)}, u32[]{:S(2)}, u32[]{:S(2)}) collective-permute-start(bf16[2,4,96,768]{3,2,1,0:T(8,128)(2,1)} %get-tuple-element.40), channel_id=1, source_target_pairs={{0,64},{16,80},{32,96},{48,112},{64,0},{80,16},{96,32},{112,48},{1... | collective-permute-start | bytes 3538952 | tf_op jit(solution)/shard_map/ppermute | solution.py:629
  68.2 34.8 %collective-permute-start.3 = (bf16[2,4,96,768]{3,2,1,0:T(8,128)(2,1)}, bf16[2,4,96,768]{3,2,1,0:T(8,128)(2,1)}, u32[]{:S(2)}, u32[]{:S(2)}) collective-permute-start(bf16[2,4,96,768]{3,2,1,0:T(8,128)(2,1)} %get-tuple-element.42), channel_id=1, source_target_pairs={{0,8},{1,9},{2,10},{3,11},{4,12},{5,13},{6,14},{7,15},{8,0},{9,1},... | collective-permute-start | bytes 3538952 | tf_op jit(solution)/shard_map/ppermute | solution.py:625
  83.9 59.0 %collective-permute-start = (bf16[2,512,768]{2,1,0:T(8,128)(2,1)}, bf16[2,512,768]{2,1,0:T(8,128)(2,1)S(1)}, u32[]{:S(2)}, u32[]{:S(2)}) collective-permute-start(bf16[2,512,768]{2,1,0:T(8,128)(2,1)} %get-tuple-element.35), channel_id=1, source_target_pairs={{1,0},{2,1},{3,2},{4,3},{5,4},{6,5},{7,6},{8,7},{9,8},{10,9},{11,1... | collective-permute-start | bytes 4718600 | tf_op jit(solution)/shard_map/ppermute | solution.py:701
  86.3 56.6 %collective-permute-start.1 = (bf16[2,512,768]{2,1,0:T(8,128)(2,1)}, bf16[2,512,768]{2,1,0:T(8,128)(2,1)S(1)}, u32[]{:S(2)}, u32[]{:S(2)}) collective-permute-start(bf16[2,512,768]{2,1,0:T(8,128)(2,1)} %get-tuple-element.36), channel_id=1, source_target_pairs={{0,1},{1,2},{2,3},{3,4},{4,5},{5,6},{6,7},{7,8},{8,9},{9,10},{10,1... | collective-permute-start | bytes 4718600 | tf_op jit(solution)/shard_map/ppermute | solution.py:702
  142.9 1.2 copy-start
  142.9 1.6 %copy-start.1 = (bf16[2,512,768]{2,1,0:T(8,128)(2,1)}, bf16[2,512,768]{2,1,0:T(8,128)(2,1)S(1)}, u32[]{:S(2)}) copy-start(bf16[2,512,768]{2,1,0:T(8,128)(2,1)S(1)} %collective-permute-done.1.behind0) | copy-start | bytes 4718596
  144.6 7.2 %copy-start.2 = (f32[12,3072]{1,0:T(8,128)S(1)}, f32[12,3072]{1,0:T(8,128)}, u32[]{:S(2)}) copy-start(f32[12,3072]{1,0:T(8,128)} %get-tuple-element.55) | copy-start | bytes 442372

commit v4 on v3

--- a/solution.py
+++ b/solution.py
@@ -107,6 +107,7 @@
         self.sends = (ctx < 15, ctx > 0)
         self.gets = (ctx > 0, ctx < 15)
         self.passes = (ctx == 0, ctx == 15)
+        self.far = (ctx == 7, ctx == 8)
 
     def start(self):
         for i in range(2):
@@ -114,6 +115,15 @@
             def _():
                 for copy in self.pieces[i]:
                     copy.start()
+
+            @pl.when(self.sends[i] & jnp.logical_not(self.far[i]))
+            def _():
+                self.straight[i].start()
+
+    def start_far(self):
+        for i in range(2):
+            @pl.when(self.far[i])
+            def _():
                 self.straight[i].start()
 
     def relay(self, *numbers):
@@ -300,6 +310,7 @@
             onward(part, block, j + 1)
             to_sibling(part, block)
         wgrad_group((z + j + 1) % 4, j + 1)
+    halo.start_far()
     halo.relay(0)
     stores = []
     for j, (src, dst) in enumerate(((keep_a, keep_a_out), (send_a, send_a_out),
@@ -392,6 +403,7 @@
             copy.start()
             first.append(copy)
     halo.start()
+    halo.start_far()
     for copy in first:
         copy.wait_recv()
     for keep, got, more, total_ref in (

time: 153 us -> 155 us (1.013)
  starting transfers between devices: 6.62 us -> 8.48 us
    pallas_call x1, Pallas kernels: 66.3 us -> 64 us  [shards(): pl.pallas_call(gather_kernel, out_shape=(pair, pair, jax.ShapeDtypeStruct...]
where the time goes in v4:
time: 155 us; the launch traced here: 153 us
  Pallas kernels  140 us (90%)
  starting transfers between devices  8.48 us (5%)
  local copies, waits for them, and re-layouts  3.72 us (2%)
    pallas_call x1, Pallas kernels, shards(): pl.pallas_call(gather_kernel, out_shape=(pair, pair, jax.ShapeDtypeStruct...  64 us
    pallas_call x1, Pallas kernels, shards(): pl.pallas_call(scatter_kernel, out_shape=(jax.ShapeDtypeStruct((ROWS, D),...  41.3 us
    pallas_call x2, Pallas kernels, shards(): pl.pallas_call(functools.partial(attention_kernel, first), out_shape=(own...  27.8 us
    pallas_call x1, Pallas kernels, shards(): pl.pallas_call(combine_kernel, out_shape=(own16, own16), grid=(4,), in_sp...  7.2 us
    unnamed x13, local copies, waits for them, and re-layouts  3.72 us
  transfers between devices with their start and end apart: 4, of which 0 were waited for; matrix products, arithmetic and copies ran while one was open for 1% of the time, Pallas kernels for 45%

profile of v4, /device:TPU:4, one launch (start us, length us, event | category | flops | bytes accessed | tf_op | source)
XLA Modules:
  0.0 153.2 jit_solution(1609365991035754893)
XLA Ops:
  0.6 0.0 copy-start.3
  0.6 0.0 copy-start.4
  0.7 64.0 %gather.1 = (bf16[2,512,1536]{2,1,0:T(8,128)(2,1)}, bf16[2,512,1536]{2,1,0:T(8,128)(2,1)}, bf16[512,1536]{1,0:T(8,128)(2,1)}, bf16[2,4,96,768]{3,2,1,0:T(8,128)(...) custom-call(bf16[12,3072]{1,0:T(8,128)(2,1)} %strip.1, ...), custom_call_target="tpu_custom_call" | custom-call | flops 10000000000 | bytes 20000000 | tf_op jit(solution)/shard_map/gather/pallas_call | solution.py:651
  64.6 1.8 %collective-permute-start.2 = (bf16[2,4,96,768]{3,2,1,0:T(8,128)(2,1)}, bf16[2,4,96,768]{3,2,1,0:T(8,128)(2,1)}, u32[]{:S(2)}, u32[]{:S(2)}) collective-permute-start(bf16[2,4,96,768]{3,2,1,0:T(8,128)(2,1)} %get-tuple-element.40), channel_id=1, source_target_pairs={{0,64},{16,80},{32,96},{48,112},{64,0},{80,16},{96,32},{112,48},{1... | collective-permute-start | bytes 3538952 | tf_op jit(solution)/shard_map/ppermute | solution.py:641
  66.4 2.0 %collective-permute-start.3 = (bf16[2,4,96,768]{3,2,1,0:T(8,128)(2,1)}, bf16[2,4,96,768]{3,2,1,0:T(8,128)(2,1)}, u32[]{:S(2)}, u32[]{:S(2)}) collective-permute-start(bf16[2,4,96,768]{3,2,1,0:T(8,128)(2,1)} %get-tuple-element.42), channel_id=1, source_target_pairs={{0,8},{1,9},{2,10},{3,11},{4,12},{5,13},{6,14},{7,15},{8,0},{9,1},... | collective-permute-start | bytes 3538952 | tf_op jit(solution)/shard_map/ppermute | solution.py:637
  68.4 0.0 copy-done.3
  68.4 0.7 copy.19.extents
  69.1 0.0 copy-done.4
  69.1 0.7 copy.18.coords
  69.8 12.8 %attention.2 = (bf16[512,1536]{1,0:T(8,128)(2,1)}, f32[512,1536]{1,0:T(8,128)}, f32[512,1536]{1,0:T(8,128)}, bf16[2,512,768]{2,1,0:T(8,128)(2,1)}, bf16[2,512,768]{2,1,0:T(8,128)(2,1)}) custom-call(s32[64,3]{1,0:T(8,128)} %copy.18.coords, s32[12,3]{1,0:T(8,128)} %copy.19.extents, bf16[512,1536]{1,0:T(8,128)(2,1)} %bitcast.9, bf16[512,1536]{1,0:T(8,128)(2,1)} %bitcast.12, ...), custom_call_target="tpu_custom_call" | custom-call | flops 6000000000 | bytes 15000000 | tf_op jit(solution)/shard_map/attention/pallas_call | solution.py:689
  82.6 2.8 %collective-permute-start = (bf16[2,512,768]{2,1,0:T(8,128)(2,1)}, bf16[2,512,768]{2,1,0:T(8,128)(2,1)S(1)}, u32[]{:S(2)}, u32[]{:S(2)}) collective-permute-start(bf16[2,512,768]{2,1,0:T(8,128)(2,1)} %get-tuple-element.35), channel_id=1, source_target_pairs={{1,0},{2,1},{3,2},{4,3},{5,4},{6,5},{7,6},{8,7},{9,8},{10,9},{11,1... | collective-permute-start | bytes 4718600 | tf_op jit(solution)/shard_map/ppermute | solution.py:713
  85.4 1.9 %collective-permute-start.1 = (bf16[2,512,768]{2,1,0:T(8,128)(2,1)}, bf16[2,512,768]{2,1,0:T(8,128)(2,1)S(1)}, u32[]{:S(2)}, u32[]{:S(2)}) collective-permute-start(bf16[2,512,768]{2,1,0:T(8,128)(2,1)} %get-tuple-element.36), channel_id=1, source_target_pairs={{0,1},{1,2},{2,3},{3,4},{4,5},{5,6},{6,7},{7,8},{8,9},{9,10},{10,1... | collective-permute-start | bytes 4718600 | tf_op jit(solution)/shard_map/ppermute | solution.py:714
  87.4 15.0 %attention.3 = (bf16[512,1536]{1,0:T(8,128)(2,1)}, f32[512,1536]{1,0:T(8,128)}, f32[512,1536]{1,0:T(8,128)}, bf16[2,512,768]{2,1,0:T(8,128)(2,1)}, bf16[2,512,768]{2,1,0:T(8,128)(2,1)}) custom-call(s32[64,3]{1,0:T(8,128)} %copy.18.coords, s32[12,3]{1,0:T(8,128)} %copy.19.extents, ...), custom_call_target="tpu_custom_call", output_to_operand_aliasing={{0}: (12, {}), {1}: (13, {}), {2}: (14, {})} | custom-call | flops 6000000000 | bytes 15000000 | tf_op jit(solution)/shard_map/attention/pallas_call | solution.py:689
  102.3 0.0 collective-permute-done.2.got_a_in
  102.3 0.0 collective-permute-done.3.got_b_in
  102.4 41.3 %scatter.1 = (f32[12,3072]{1,0:T(8,128)}, bf16[2,512,768]{2,1,0:T(8,128)(2,1)}, bf16[2,512,768]{2,1,0:T(8,128)(2,1)}) custom-call(bf16[2,512,768]{2,1,0:T(8,128)(2,1)} %get-tuple-element.37.to_prev, bf16[2,512,768]{2,1,0:T(8,128)(2,1)} %get-tuple-element.38.to_next, bf16[2,4,96,768]{3,2,1,0:T(8,128)(2,1)} %get-tuple-element.39.keep_a_in, ...), custom_call_target="tpu_custom_call" | custom-call | flops 10000000000 | bytes 20000000 | tf_op jit(solution)/shard_map/scatter/pallas_call | solution.py:716
  143.6 0.0 collective-permute-done.ahead0
  143.6 0.0 copy-start
  143.6 0.0 collective-permute-done.1.behind0
  143.7 0.0 copy-start.1
  143.7 1.1 copy-done
  144.8 0.5 copy-done.1
  145.3 0.0 copy-start.2
  145.3 7.2 %combine.1 = (bf16[512,1536]{1,0:T(8,128)(2,1)}, bf16[512,1536]{1,0:T(8,128)(2,1)}) custom-call(f32[512,1536]{1,0:T(8,128)} %get-tuple-element.33.dk, f32[512,1536]{1,0:T(8,128)} %get-tuple-element.34.dv, bf16[2,512,768]{2,1,0:T(8,128)(2,1)} %copy-done, bf16[2,512,768]{2,1,0:T(8,128)(2,1)} %copy-done.1, bf16[2,512,768]{2,1,0:T(8,128)(2,1)} %get-tuple-element.43.ahead1, ...), custom_call_target="tpu_custom_call" | custom-call | tf_op jit(solution)/shard_map/combine/pallas_call | solution.py:740
  152.5 0.0 copy-done.2
  152.5 0.7 copy.24
Async XLA Ops:
  0.6 67.8 %copy-start.3 = (s32[12,3]{0,1:T(4,128)S(1)}, s32[12,3]{0,1:T(4,128)}, u32[]{:S(2)}) copy-start(s32[12,3]{0,1:T(4,128)} %param.17) | copy-start | bytes 436
  0.6 68.4 %copy-start.4 = (s32[64,3]{0,1:T(4,128)S(1)}, s32[64,3]{0,1:T(4,128)}, u32[]{:S(2)}) copy-start(s32[64,3]{0,1:T(4,128)} %param.16) | copy-start | bytes 2308
  64.6 37.7 %collective-permute-start.2 = (bf16[2,4,96,768]{3,2,1,0:T(8,128)(2,1)}, bf16[2,4,96,768]{3,2,1,0:T(8,128)(2,1)}, u32[]{:S(2)}, u32[]{:S(2)}) collective-permute-start(bf16[2,4,96,768]{3,2,1,0:T(8,128)(2,1)} %get-tuple-element.40), channel_id=1, source_target_pairs={{0,64},{16,80},{32,96},{48,112},{64,0},{80,16},{96,32},{112,48},{1... | collective-permute-start | bytes 3538952 | tf_op jit(solution)/shard_map/ppermute | solution.py:641
  66.4 35.9 %collective-permute-start.3 = (bf16[2,4,96,768]{3,2,1,0:T(8,128)(2,1)}, bf16[2,4,96,768]{3,2,1,0:T(8,128)(2,1)}, u32[]{:S(2)}, u32[]{:S(2)}) collective-permute-start(bf16[2,4,96,768]{3,2,1,0:T(8,128)(2,1)} %get-tuple-element.42), channel_id=1, source_target_pairs={{0,8},{1,9},{2,10},{3,11},{4,12},{5,13},{6,14},{7,15},{8,0},{9,1},... | collective-permute-start | bytes 3538952 | tf_op jit(solution)/shard_map/ppermute | solution.py:637
  82.6 61.0 %collective-permute-start = (bf16[2,512,768]{2,1,0:T(8,128)(2,1)}, bf16[2,512,768]{2,1,0:T(8,128)(2,1)S(1)}, u32[]{:S(2)}, u32[]{:S(2)}) collective-permute-start(bf16[2,512,768]{2,1,0:T(8,128)(2,1)} %get-tuple-element.35), channel_id=1, source_target_pairs={{1,0},{2,1},{3,2},{4,3},{5,4},{6,5},{7,6},{8,7},{9,8},{10,9},{11,1... | collective-permute-start | bytes 4718600 | tf_op jit(solution)/shard_map/ppermute | solution.py:713
  85.4 58.2 %collective-permute-start.1 = (bf16[2,512,768]{2,1,0:T(8,128)(2,1)}, bf16[2,512,768]{2,1,0:T(8,128)(2,1)S(1)}, u32[]{:S(2)}, u32[]{:S(2)}) collective-permute-start(bf16[2,512,768]{2,1,0:T(8,128)(2,1)} %get-tuple-element.36), channel_id=1, source_target_pairs={{0,1},{1,2},{2,3},{3,4},{4,5},{5,6},{6,7},{7,8},{8,9},{9,10},{10,1... | collective-permute-start | bytes 4718600 | tf_op jit(solution)/shard_map/ppermute | solution.py:714
  143.6 1.2 copy-start
  143.7 1.6 %copy-start.1 = (bf16[2,512,768]{2,1,0:T(8,128)(2,1)}, bf16[2,512,768]{2,1,0:T(8,128)(2,1)S(1)}, u32[]{:S(2)}) copy-start(bf16[2,512,768]{2,1,0:T(8,128)(2,1)S(1)} %collective-permute-done.1.behind0) | copy-start | bytes 4718596
  145.3 7.2 %copy-start.2 = (f32[12,3072]{1,0:T(8,128)S(1)}, f32[12,3072]{1,0:T(8,128)}, u32[]{:S(2)}) copy-start(f32[12,3072]{1,0:T(8,128)} %get-tuple-element.55) | copy-start | bytes 442372

commit v5 on v4

--- a/solution.py
+++ b/solution.py
@@ -157,7 +157,7 @@
 def gather_kernel(
     strip, keys, vals, so_hbm, og_hbm,
     before, after, d_attn_out, keep_a_out, send_a_out, keep_b_out, send_b_out,
-    padded, strips, full, so, og, so_sib, og_sib, turn, d_attn, keep_a, send_a, keep_b, send_b,
+    padded, strips, full, so, og, so_sib, og_sib, turn, d_attn, partial, keep_a, send_a, keep_b, send_b,
     strip_send, strip_recv, near_send, far_send, pass_send, ag_recv, late_recv, sib_send, sib_recv,
     ex_send, ex_recv, load_sem, store_sem, *halo_sems,
 ):
@@ -332,32 +332,44 @@
                 to_sibling(part, block)
         if j:
             halo.relay(j)
-    for inner in (0,) + STEPS:
+    def from_sibling(part, group):
+        for inner in range(4):
+            block = group * 4 + inner
+            remote(piece(1 - c, block, part), piece(1 - c, block, part),
+                   sib_send.at[part, block], sib_recv.at[part, block], sib).wait_recv()
+
+    def project(part, group):
+        low, high = PARTS[part]
+        feats = pl.ds(pl.multiple_of(group * 4 * BLK, 4 * BLK), 4 * BLK)
+
+        def some_rows(i, carry):
+            rows = pl.ds(pl.multiple_of(i * 256, 256), 256)
+            total = jnp.zeros((256, 4 * BLK), F32) if part == 0 else partial[rows, feats]
+            for h in range(2):
+                weight = full[h, pl.ds(group * 4, 4), :, low:high].reshape(4 * BLK, high - low)
+                total += lax.dot_general(og[rows, h * HALF + low:h * HALF + high], weight, NT,
+                                         preferred_element_type=F32)
+            if part == 0:
+                partial[rows, feats] = total
+            else:
+                d_attn[rows, feats] = total.astype(BF16)
+            return carry
+
+        from_sibling(part, group)
+        lax.fori_loop(0, TOK // 256, some_rows, 0)
+
+    for i, inner in enumerate((0,) + STEPS):
+        if i < 3:
+            project(0, (z + (0, 1, 3)[i]) % 4)
         for part in range(2):
             block = far_block(part, 2, inner)
             arrived_late(part, block)
             to_sibling(part, block)
-
+    project(0, (z + 2) % 4)
     for step in (0,) + STEPS:
         group = (z + step) % 4
-        for inner in range(4):
-            block = group * 4 + inner
-            for part in range(2):
-                remote(piece(1 - c, block, part), piece(1 - c, block, part),
-                       sib_send.at[part, block], sib_recv.at[part, block], sib).wait_recv()
+        project(1, group)
         feats = pl.ds(pl.multiple_of(group * 4 * BLK, 4 * BLK), 4 * BLK)
-
-        def project(i, carry):
-            rows = pl.ds(pl.multiple_of(i * 256, 256), 256)
-            total = jnp.zeros((256, 4 * BLK), F32)
-            for h in range(2):
-                weight = full[h, pl.ds(group * 4, 4)].reshape(4 * BLK, HALF)
-                total += lax.dot_general(og[rows, h * HALF:(h + 1) * HALF], weight, NT,
-                                         preferred_element_type=F32)
-            d_attn[rows, feats] = total.astype(BF16)
-            return carry
-
-        lax.fori_loop(0, TOK // 256, project, 0)
         stores.append(pltpu.make_async_copy(d_attn.at[:, feats], d_attn_out.at[:, feats],
                                             store_sem.at[4 + step]))
         stores[-1].start()
@@ -403,7 +415,6 @@
             copy.start()
             first.append(copy)
     halo.start()
-    halo.start_far()
     for copy in first:
         copy.wait_recv()
     for keep, got, more, total_ref in (
@@ -422,6 +433,7 @@
             copy = remote(src, dst, second_send.at[part, i], second_recv.at[part, i], target)
             copy.start()
             second.append(copy)
+    halo.start_far()
     halo.relay(0, 1)
     for copy in second:
         copy.wait_recv()
@@ -663,6 +675,7 @@
             pltpu.VMEM((TOK, HALF), BF16),
             pltpu.VMEM((4, BLK, SUM_CUT), BF16),
             pltpu.VMEM((TOK, HD), BF16),
+            pltpu.VMEM((TOK, HD), F32),
         ] + [pltpu.VMEM((2, 4, BLK, SUM_CUT), BF16)] * 4 + [
             dma((7,)), dma((8,)), dma((2, 3)), dma((2, 4, 2)), dma((2, 4, 2)), dma((2, 16)),
             dma((2, 16)), dma((2, 16)), dma((2, 16)), dma((2,)), dma((2,)), dma((2,)), dma((8,)),

time: 155 us -> 151 us (0.974)
  Pallas kernels: 140 us -> 135 us
    pallas_call x1, Pallas kernels: 41.3 us -> 36.9 us  [shards(): pl.pallas_call(scatter_kernel, out_shape=(jax.ShapeDtypeStruct((ROWS, D),...]
    ppermute x1, starting transfers between devices: 2.81 us -> 4.8 us  [shards(): ahead = lax.ppermute(towards[0][0], 'ctx', [(i + 1, i) for i in range(15)])]
  transfers between devices with their start and end apart: 4 -> 4, of which waited for: 0 -> 0; matrix products, arithmetic and copies ran while one was open for 1% -> 1% of each run, Pallas kernels for 45% -> 44%
where the time goes in v5:
time: 151 us; the launch traced here: 148 us
  Pallas kernels  135 us (89%)
  starting transfers between devices  9.21 us (6%)
  local copies, waits for them, and re-layouts  3.72 us (2%)
    pallas_call x1, Pallas kernels, shards(): pl.pallas_call(gather_kernel, out_shape=(pair, pair, jax.ShapeDtypeStruct...  62.5 us
    pallas_call x1, Pallas kernels, shards(): pl.pallas_call(scatter_kernel, out_shape=(jax.ShapeDtypeStruct((ROWS, D),...  36.9 us
    pallas_call x2, Pallas kernels, shards(): pl.pallas_call(functools.partial(attention_kernel, first), out_shape=(own...  28.2 us
    pallas_call x1, Pallas kernels, shards(): pl.pallas_call(combine_kernel, out_shape=(own16, own16), grid=(4,), in_sp...  7.2 us
    ppermute x1, starting transfers between devices, shards(): ahead = lax.ppermute(towards[0][0], 'ctx', [(i + 1, i) for i in range(15)])  4.8 us
    unnamed x13, local copies, waits for them, and re-layouts  3.72 us
  transfers between devices with their start and end apart: 4, of which 0 were waited for; matrix products, arithmetic and copies ran while one was open for 1% of the time, Pallas kernels for 44%

profile of v5, /device:TPU:4, one launch (start us, length us, event | category | flops | bytes accessed | tf_op | source)
XLA Modules:
  0.0 148.5 jit_solution(16361451296094773578)
XLA Ops:
  0.6 0.0 copy-start.3
  0.6 0.0 copy-start.4
  0.7 62.5 %gather.1 = (bf16[2,512,1536]{2,1,0:T(8,128)(2,1)}, bf16[2,512,1536]{2,1,0:T(8,128)(2,1)}, bf16[512,1536]{1,0:T(8,128)(2,1)}, bf16[2,4,96,768]{3,2,1,0:T(8,128)(...) custom-call(bf16[12,3072]{1,0:T(8,128)(2,1)} %strip.1, ...), custom_call_target="tpu_custom_call" | custom-call | flops 10000000000 | bytes 20000000 | tf_op jit(solution)/shard_map/gather/pallas_call | solution.py:663
  63.1 1.8 %collective-permute-start.2 = (bf16[2,4,96,768]{3,2,1,0:T(8,128)(2,1)}, bf16[2,4,96,768]{3,2,1,0:T(8,128)(2,1)}, u32[]{:S(2)}, u32[]{:S(2)}) collective-permute-start(bf16[2,4,96,768]{3,2,1,0:T(8,128)(2,1)} %get-tuple-element.40), channel_id=1, source_target_pairs={{0,64},{16,80},{32,96},{48,112},{64,0},{80,16},{96,32},{112,48},{1... | collective-permute-start | bytes 3538952 | tf_op jit(solution)/shard_map/ppermute | solution.py:653
  64.9 0.7 collective-permute-start.3
  65.6 0.0 copy-done.3
  65.6 0.7 copy.19.extents
  66.3 0.0 copy-done.4
  66.3 0.7 copy.18.coords
  67.0 13.3 %attention.2 = (bf16[512,1536]{1,0:T(8,128)(2,1)}, f32[512,1536]{1,0:T(8,128)}, f32[512,1536]{1,0:T(8,128)}, bf16[2,512,768]{2,1,0:T(8,128)(2,1)}, bf16[2,512,768]{2,1,0:T(8,128)(2,1)}) custom-call(s32[64,3]{1,0:T(8,128)} %copy.18.coords, s32[12,3]{1,0:T(8,128)} %copy.19.extents, bf16[512,1536]{1,0:T(8,128)(2,1)} %bitcast.9, bf16[512,1536]{1,0:T(8,128)(2,1)} %bitcast.12, ...), custom_call_target="tpu_custom_call" | custom-call | flops 6000000000 | bytes 15000000 | tf_op jit(solution)/shard_map/attention/pallas_call | solution.py:702
  80.3 4.8 %collective-permute-start = (bf16[2,512,768]{2,1,0:T(8,128)(2,1)}, bf16[2,512,768]{2,1,0:T(8,128)(2,1)S(1)}, u32[]{:S(2)}, u32[]{:S(2)}) collective-permute-start(bf16[2,512,768]{2,1,0:T(8,128)(2,1)} %get-tuple-element.35), channel_id=1, source_target_pairs={{1,0},{2,1},{3,2},{4,3},{5,4},{6,5},{7,6},{8,7},{9,8},{10,9},{11,1... | collective-permute-start | bytes 4718600 | tf_op jit(solution)/shard_map/ppermute | solution.py:726
  85.1 1.9 %collective-permute-start.1 = (bf16[2,512,768]{2,1,0:T(8,128)(2,1)}, bf16[2,512,768]{2,1,0:T(8,128)(2,1)S(1)}, u32[]{:S(2)}, u32[]{:S(2)}) collective-permute-start(bf16[2,512,768]{2,1,0:T(8,128)(2,1)} %get-tuple-element.36), channel_id=1, source_target_pairs={{0,1},{1,2},{2,3},{3,4},{4,5},{5,6},{6,7},{7,8},{8,9},{9,10},{10,1... | collective-permute-start | bytes 4718600 | tf_op jit(solution)/shard_map/ppermute | solution.py:727
  87.0 14.9 %attention.3 = (bf16[512,1536]{1,0:T(8,128)(2,1)}, f32[512,1536]{1,0:T(8,128)}, f32[512,1536]{1,0:T(8,128)}, bf16[2,512,768]{2,1,0:T(8,128)(2,1)}, bf16[2,512,768]{2,1,0:T(8,128)(2,1)}) custom-call(s32[64,3]{1,0:T(8,128)} %copy.18.coords, s32[12,3]{1,0:T(8,128)} %copy.19.extents, ...), custom_call_target="tpu_custom_call", output_to_operand_aliasing={{0}: (12, {}), {1}: (13, {}), {2}: (14, {})} | custom-call | flops 6000000000 | bytes 15000000 | tf_op jit(solution)/shard_map/attention/pallas_call | solution.py:702
  101.9 0.0 collective-permute-done.2.got_a_in
  102.0 0.0 collective-permute-done.3.got_b_in
  102.0 36.9 %scatter.1 = (f32[12,3072]{1,0:T(8,128)}, bf16[2,512,768]{2,1,0:T(8,128)(2,1)}, bf16[2,512,768]{2,1,0:T(8,128)(2,1)}) custom-call(bf16[2,512,768]{2,1,0:T(8,128)(2,1)} %get-tuple-element.37.to_prev, bf16[2,512,768]{2,1,0:T(8,128)(2,1)} %get-tuple-element.38.to_next, bf16[2,4,96,768]{3,2,1,0:T(8,128)(2,1)} %get-tuple-element.39.keep_a_in, ...), custom_call_target="tpu_custom_call" | custom-call | flops 10000000000 | bytes 20000000 | tf_op jit(solution)/shard_map/scatter/pallas_call | solution.py:729
  138.9 0.0 collective-permute-done.ahead0
  138.9 0.0 copy-start
  138.9 0.0 collective-permute-done.1.behind0
  138.9 0.0 copy-start.1
  139.0 1.1 copy-done
  140.1 0.5 copy-done.1
  140.6 0.0 copy-start.2
  140.6 7.2 %combine.1 = (bf16[512,1536]{1,0:T(8,128)(2,1)}, bf16[512,1536]{1,0:T(8,128)(2,1)}) custom-call(f32[512,1536]{1,0:T(8,128)} %get-tuple-element.33.dk, f32[512,1536]{1,0:T(8,128)} %get-tuple-element.34.dv, bf16[2,512,768]{2,1,0:T(8,128)(2,1)} %copy-done, bf16[2,512,768]{2,1,0:T(8,128)(2,1)} %copy-done.1, bf16[2,512,768]{2,1,0:T(8,128)(2,1)} %get-tuple-element.43.ahead1, ...), custom_call_target="tpu_custom_call" | custom-call | tf_op jit(solution)/shard_map/combine/pallas_call | solution.py:753
  147.8 0.0 copy-done.2
  147.8 0.7 copy.24
Async XLA Ops:
  0.6 65.0 %copy-start.3 = (s32[12,3]{0,1:T(4,128)S(1)}, s32[12,3]{0,1:T(4,128)}, u32[]{:S(2)}) copy-start(s32[12,3]{0,1:T(4,128)} %param.17) | copy-start | bytes 436
  0.6 65.7 %copy-start.4 = (s32[64,3]{0,1:T(4,128)S(1)}, s32[64,3]{0,1:T(4,128)}, u32[]{:S(2)}) copy-start(s32[64,3]{0,1:T(4,128)} %param.16) | copy-start | bytes 2308
  63.1 38.8 %collective-permute-start.2 = (bf16[2,4,96,768]{3,2,1,0:T(8,128)(2,1)}, bf16[2,4,96,768]{3,2,1,0:T(8,128)(2,1)}, u32[]{:S(2)}, u32[]{:S(2)}) collective-permute-start(bf16[2,4,96,768]{3,2,1,0:T(8,128)(2,1)} %get-tuple-element.40), channel_id=1, source_target_pairs={{0,64},{16,80},{32,96},{48,112},{64,0},{80,16},{96,32},{112,48},{1... | collective-permute-start | bytes 3538952 | tf_op jit(solution)/shard_map/ppermute | solution.py:653
  64.9 37.1 %collective-permute-start.3 = (bf16[2,4,96,768]{3,2,1,0:T(8,128)(2,1)}, bf16[2,4,96,768]{3,2,1,0:T(8,128)(2,1)}, u32[]{:S(2)}, u32[]{:S(2)}) collective-permute-start(bf16[2,4,96,768]{3,2,1,0:T(8,128)(2,1)} %get-tuple-element.42), channel_id=1, source_target_pairs={{0,8},{1,9},{2,10},{3,11},{4,12},{5,13},{6,14},{7,15},{8,0},{9,1},... | collective-permute-start | bytes 3538952 | tf_op jit(solution)/shard_map/ppermute | solution.py:649
  80.3 58.6 %collective-permute-start = (bf16[2,512,768]{2,1,0:T(8,128)(2,1)}, bf16[2,512,768]{2,1,0:T(8,128)(2,1)S(1)}, u32[]{:S(2)}, u32[]{:S(2)}) collective-permute-start(bf16[2,512,768]{2,1,0:T(8,128)(2,1)} %get-tuple-element.35), channel_id=1, source_target_pairs={{1,0},{2,1},{3,2},{4,3},{5,4},{6,5},{7,6},{8,7},{9,8},{10,9},{11,1... | collective-permute-start | bytes 4718600 | tf_op jit(solution)/shard_map/ppermute | solution.py:726
  85.1 53.8 %collective-permute-start.1 = (bf16[2,512,768]{2,1,0:T(8,128)(2,1)}, bf16[2,512,768]{2,1,0:T(8,128)(2,1)S(1)}, u32[]{:S(2)}, u32[]{:S(2)}) collective-permute-start(bf16[2,512,768]{2,1,0:T(8,128)(2,1)} %get-tuple-element.36), channel_id=1, source_target_pairs={{0,1},{1,2},{2,3},{3,4},{4,5},{5,6},{6,7},{7,8},{8,9},{9,10},{10,1... | collective-permute-start | bytes 4718600 | tf_op jit(solution)/shard_map/ppermute | solution.py:727
  138.9 1.2 copy-start
  138.9 1.6 %copy-start.1 = (bf16[2,512,768]{2,1,0:T(8,128)(2,1)}, bf16[2,512,768]{2,1,0:T(8,128)(2,1)S(1)}, u32[]{:S(2)}) copy-start(bf16[2,512,768]{2,1,0:T(8,128)(2,1)S(1)} %collective-permute-done.1.behind0) | copy-start | bytes 4718596
  140.6 7.2 %copy-start.2 = (f32[12,3072]{1,0:T(8,128)S(1)}, f32[12,3072]{1,0:T(8,128)}, u32[]{:S(2)}) copy-start(f32[12,3072]{1,0:T(8,128)} %get-tuple-element.55) | copy-start | bytes 442372
